TPU v7x, 128 devices: a whole 4x4x4 slice. The times are simulated.
128 devices in a mesh: prow: 16 (over x, y), pcol: 8 (over z, core).
Axes of the slice: x: 4, y: 4, z: 4, core: 2. Of those that a mesh axis runs over, the one named last changes fastest.
Arguments:
- trailing: float32 [16384, 16384], P('prow', 'pcol'), may hold values from -6 to 6
- factors: float32 [64, 16384], P(None, ('prow', 'pcol')), may hold values from -1 to 1
- pivots: int32 [64], replicated, may hold values from 0 to 16383, as said below
Outputs:
- updated: float32 [16384, 16384], P('prow', 'pcol')
Inputs may be any that keep to these rules, and one draw needn't show every extreme that they name: Entry j of pivots is j or larger.
All inputs are finite; a program needn't handle non-finite values.
Results may differ from a plain program's by a relative error of at most 0.000064.
Values sent between devices are 32-bit elements; how exact they have to be, the bound alone decides.
No kernel may reach another device: no remote copies, remote signals or barrier semaphores. Data moves between devices by JAX's collectives and lax.ppermute only.
A program may use at most 64 MiB of HBM per device.

v0:
```python
import jax
import jax.numpy as jnp
from jax import lax
from jax.sharding import PartitionSpec as P


def broadcast(value, axis, source):
    kept = jnp.where(lax.axis_index(axis) == source, value, 0).astype(value.dtype)
    return lax.psum(kept, axis)


def holder_of(matrix_row, width, groups):
    return matrix_row // width % groups


def local_of(matrix_row, width, groups):
    return matrix_row // (width * groups) * width + matrix_row % width


def solve_top(unit_lower, top_rows):
    return jax.scipy.linalg.solve_triangular(unit_lower, top_rows, lower=True, unit_diagonal=True)


def swap_sources(changed, width):
    slots = changed.shape[0]
    slot_ids = jnp.arange(slots, dtype=jnp.int32)
    same_row = changed[:, None] == changed[None, :]
    canonical = jnp.min(jnp.where(same_row, slot_ids[None, :], slots), axis=1)
    first_hot = (canonical[:width, None] == slot_ids[None, :]).astype(jnp.float32)
    second_hot = (canonical[width:, None] == slot_ids[None, :]).astype(jnp.float32)
    identity = jnp.eye(slots, dtype=jnp.float32)
    swaps = (
        identity[None, :, :]
        - first_hot[:, :, None] * first_hot[:, None, :]
        - second_hot[:, :, None] * second_hot[:, None, :]
    )
    swaps = (
        swaps
        + first_hot[:, :, None] * second_hot[:, None, :]
        + second_hot[:, :, None] * first_hot[:, None, :]
    )
    count = width
    while count > 1:
        swaps = jnp.einsum(
            "kij,kjl->kil", swaps[1::2], swaps[0::2], precision=lax.Precision.HIGHEST
        )
        count = count // 2
    values = jnp.dot(swaps[0], changed.astype(jnp.float32), precision=lax.Precision.HIGHEST)
    canon_hot = (canonical[:, None] == slot_ids[None, :]).astype(jnp.float32)
    spread = jnp.dot(canon_hot, values, precision=lax.Precision.HIGHEST)
    return (spread + 0.5).astype(jnp.int32)


def body(trailing, factors, pivots):
    rows_dev, cols_dev = trailing.shape
    width = factors.shape[0]
    groups = lax.axis_size("prow")
    my_row = lax.axis_index("prow")
    changed = jnp.concatenate([jnp.arange(width, dtype=jnp.int32), pivots])
    sources = swap_sources(changed, width)
    holders = holder_of(sources, width, groups)
    local_rows = local_of(sources, width, groups)
    picked = jnp.where((holders == my_row)[:, None], jnp.take(trailing, local_rows, axis=0), 0.0)
    diag_block = broadcast(factors[:, :width], ("prow", "pcol"), 0)
    unit_lower = jnp.transpose(diag_block)
    summed = lax.psum(picked, "prow")
    upper_rows = solve_top(unit_lower, summed[:width])
    displaced = summed[width:]
    targets = holder_of(pivots, width, groups)
    target_rows = jnp.where(targets == my_row, local_of(pivots, width, groups), rows_dev)
    swapped = trailing.at[target_rows].set(displaced, mode="drop")
    product = lax.dot_general(
        lax.all_gather(factors, "pcol", axis=1, tiled=True),
        upper_rows,
        (((0,), (0,)), ((), ())),
        precision=lax.Precision.HIGHEST,
        preferred_element_type=jnp.float32,
    )
    updated = swapped - product
    top_rows = jnp.where(my_row == 0, upper_rows, updated[:width])
    return lax.dynamic_update_slice(updated, top_rows, (0, 0))


def solution(mesh):
    return jax.shard_map(
        body,
        mesh=mesh,
        in_specs=(P("prow", "pcol"), P(None, ("prow", "pcol")), P()),
        out_specs=P("prow", "pcol"),
        check_vma=False,
    )
```

profile of v0, /device:TPU:0, one launch (start us, length us, event | category | flops | bytes accessed | tf_op | source)
XLA Modules:
  0.0 147.6 jit_solution(15713510142396153782)
XLA Ops:
  6.5 0.0 copy-start.2
  6.5 0.0 all-reduce.2.cloned.1.call-start
  6.5 7.9 %copy.10 = f32[1024,2048]{1,0:T(8,128)} copy(f32[1024,2048]{1,0:T(8,128)} %param.3) | data formatting | bytes 16777216
  14.5 0.0 copy-done.2
  14.5 0.1 pad_add_fusion
  14.5 0.2 select_reduce_fusion
  14.7 0.1 fusion.35
  14.8 0.1 fusion.26
  14.9 2.5 %multiply_add_fusion = f32[64,128,128]{2,1,0:T(8,128)S(1)} fusion(f32[64,128]{1,0:T(8,128)S(1)} %get-tuple-element.11, f32[64,128]{1,0:T(8,128)S(1)} %get-tuple-element.10, f32[128,128]{1,0:T(8,128)S(1)} %fusion.23), kind=kLoop, calls=%fused_computation.3 | loop fusion | flops 8388608 | bytes 4325376 | tf_op jit(solution)/shard_map/add | solution.py:38
  17.4 2.3 %fusion = f32[32,128,128]{2,1,0:T(8,128)S(1)} fusion(f32[64,128,128]{2,1,0:T(8,128)S(1)} %multiply_add_fusion), kind=kOutput, calls=%fused_computation.4 | convolution fusion | flops 805306368 | bytes 6291456 | tf_op jit(solution)/shard_map/kij,kjl->kil/dot_general | solution.py:44
  19.7 1.2 fusion.5
  20.9 0.6 fusion.13
  21.5 0.4 fusion.16
  21.9 0.3 fusion.19
  22.2 0.2 fusion.22
  22.4 0.2 convolution_bitcast_fusion.1
  22.6 0.3 compare_and_fusion
  22.9 0.0 copy-start.1
  22.9 4.8 %gather_fusion = f32[128,2048]{1,0:T(8,128)S(1)} fusion(f32[1024,2048]{1,0:T(8,128)} %copy.10, s32[1024]{0:T(1024)S(1)} %pad_clamp_fusion), kind=kCustom, calls=%fused_computation | custom fusion | bytes 2097664 | tf_op jit(solution)/shard_map/jit(_take)/gather | solution.py:63
  27.8 1.2 select_select_fusion
  29.0 0.0 all-reduce.2.cloned.1.call-update
  29.1 0.0 copy-done.1
  29.1 69.4 %psum.15 = f32[64,64]{0,1:T(8,128)S(1)} all-reduce(f32[64,64]{0,1:T(8,128)S(1)} %select_bitcast_fusion), channel_id=1, replica_groups=mesh['prow'=16,'pcol'=8] {'prow','pcol'}, use_global_device_ids=true, to_apply=%region_3.4 | all-reduce | flops 4096 | bytes 32768 | tf_op jit(solution)/shard_map/psum | solution.py:9
  98.5 0.1 copy.5
  98.6 0.1 add_bitcast_fusion
  98.6 4.9 %custom-call.4 = f32[1,64,64]{1,2,0:T(8,128)S(1)} custom-call(f32[1,64,64]{2,1,0:T(8,128)S(1)} %add_bitcast_fusion), custom_call_target="InvertDiagBlocksLowerTriangular" | custom-call | tf_op jit(solution)/shard_map/jit(_solve_triangular)/triangular_solve | solution.py:21
  103.5 12.8 %all_gather.3 = f32[64,1024]{1,0:T(8,128)S(1)} all-gather(f32[64,128]{1,0:T(8,128)S(1)} %copy-done.1), channel_id=1, replica_groups=mesh['prow'=16,'pcol'=8] {'pcol'}, dimensions={1}, use_global_device_ids=true | all-gather | bytes 294912 | tf_op jit(solution)/shard_map/all_gather | solution.py:73
  116.4 2.3 %all-reduce.2.cloned.1.call-done = f32[128,2048]{1,0:T(8,128)} async-done(((f32[128,2048]{1,0:T(8,128)}), f32[128,2048]{1,0:T(8,128)}) %all-reduce.2.cloned.1.call-update) | async-done | bytes 1048592 | tf_op jit(solution)/shard_map/psum | solution.py:66
  118.7 0.0 copy-start
  118.7 8.3 %scatter_custom_fusion = f32[1024,2048]{1,0:T(8,128)} fusion(f32[1024,2048]{1,0:T(8,128)} %copy.10, s32[64]{0:T(128)S(1)} %compare_select_fusion.1, f32[128,2048]{1,0:T(8,128)} %all-reduce.2.cloned.1.call-done), kind=kCustom, calls=%fused_computation.19 | custom fusion | bytes 8912896 | tf_op jit(solution)/shard_map/scatter | solution.py:71
  127.0 0.0 copy-done
  127.0 0.6 fusion.9
  127.6 11.2 %bitcast_subtract_fusion = f32[1024,2048]{1,0:T(8,128)} fusion(f32[1024,2048]{1,0:T(8,128)} %scatter_custom_fusion, f32[64,2048]{1,0:T(8,128)S(1)} %fusion.9, f32[64,1024]{1,0:T(8,128)S(1)} %all_gather.3), kind=kOutput, calls=%fused_computation.2 | convolution fusion | flops 1612709888 | bytes 17563648 | tf_op jit(solution)/shard_map/dot_general | solution.py:72
  138.8 1.9 %fusion.8 = f32[1024,2048]{1,0:T(8,128)} fusion(f32[1024,2048]{1,0:T(8,128)} %bitcast_subtract_fusion, f32[64,2048]{1,0:T(8,128)S(1)} %fusion.9, pred[]{:T(512)S(6)} %eq.114), kind=kLoop, calls=%fused_computation.16 | loop fusion | flops 131072 | bytes 1572865 | tf_op jit(solution)/shard_map/dynamic_update_slice | solution.py:81
  (6 shorter events, 0.0 us)
Async XLA Ops:
  6.5 7.9 %copy-start.2 = (s32[64]{0:T(128)S(1)}, s32[64]{0:T(128)}, u32[]{:S(2)}) copy-start(s32[64]{0:T(128)} %param.5) | copy-start | bytes 772
  6.5 112.2 %all-reduce.2.cloned.1.call-start = ((), (), s32[]{:S(2)}) async-start(), calls=%async_computation | async-start | bytes 2097152 | tf_op jit(solution)/shard_map/psum | solution.py:66
  22.9 6.1 %copy-start.1 = (f32[64,128]{1,0:T(8,128)S(1)}, f32[64,128]{1,0:T(8,128)}, u32[]{:S(2)}) copy-start(f32[64,128]{1,0:T(8,128)} %param.4) | copy-start | bytes 98308
  118.7 8.3 %copy-start = (f32[128,2048]{1,0:T(8,128)S(1)}, f32[128,2048]{1,0:T(8,128)}, u32[]{:S(2)}) copy-start(f32[128,2048]{1,0:T(8,128)} %all-reduce.2.cloned.1.call-done) | copy-start | bytes 3145732
Sparse Core Ops, SparseCore 0:
  29.2 89.5 all-reduce.1
where the time goes:
time: 148 us
  blocking collectives  82.2 us (56%)
  local copies, waits for them, and re-layouts  21.2 us (14%)
  matrix products  17.3 us (12%)
  between operations  13.6 us (9%)
  other arithmetic  11 us (7%)
  waiting for transfers between devices  2.36 us (2%)
    psum x1, blocking collectives, broadcast(): return lax.psum(kept, axis)  69.4 us
    all_gather x1, blocking collectives, body(): lax.all_gather(factors, 'pcol', axis=1, tiled=True)  12.8 us
    dot_general x1, matrix products, body(): lax.dot_general(lax.all_gather(factors, 'pcol', axis=1, tiled=True), uppe...  11.2 us
    scatter x1, local copies, waits for them, and re-layouts, body(): swapped = trailing.at[target_rows].set(displaced, mode='drop')  8.27 us
    unnamed x7, local copies, waits for them, and re-layouts  7.91 us
    dot_general x6, matrix products, swap_sources(): jnp.einsum('kij,kjl->kil', swaps[1::2], swaps[0::2], precision=lax.Precis...  4.99 us
    another operation x3, other arithmetic, solve_top(): jax.scipy.linalg.solve_triangular(unit_lower, top_rows, lower=True, unit_...  4.98 us
    gather x1, local copies, waits for them, and re-layouts, body(): jnp.take(trailing, local_rows, axis=0)  4.84 us
  transfers between devices with their start and end apart: 1, of which 1 were waited for; matrix products, arithmetic and copies ran while one was open for 3% of the time, Pallas kernels for 0%

commit v1 on v0

v1 whole, which is shorter than its diff:
```python
import functools

import jax
import jax.numpy as jnp
from jax import lax
from jax.experimental import pallas as pl
from jax.experimental.pallas import tpu as pltpu
from jax.sharding import PartitionSpec as P

LANES = 128
NB = 64
N_PROW = 16
N_PCOL = 8
ROWS = 16384
EXTRA = 64
DISPLACED = 64
LOWER = 32
SEND_ROWS = NB + EXTRA
BACK_ROWS = NB + DISPLACED + LOWER
F32 = jnp.float32
BF16 = jnp.bfloat16


def holder_of(row):
    return (row // NB) % N_PROW


def local_of(row):
    return row // (NB * N_PROW) * NB + row % NB


def pick_kernel(pivots, trailing, sent, top_from, moved, own, order, count, sem):
    me = lax.axis_index("prow")

    def touch(j, carry):
        order[pivots[j]] = pivots[j]
        return carry

    def touch_top(j, carry):
        order[j] = j
        return carry

    def swap(j, carry):
        k = pivots[j]
        a = order[j]
        b = order[k]
        order[j] = b
        order[k] = a
        return carry

    def row_copy(row, slot, piece):
        return pltpu.make_async_copy(
            trailing.at[pl.ds(row, 1), pl.ds(piece * LANES, LANES)],
            sent.at[piece, pl.ds(slot, 1), :],
            sem,
        )

    def top_copy(piece):
        return pltpu.make_async_copy(
            trailing.at[pl.ds(0, NB), pl.ds(piece * LANES, LANES)],
            sent.at[piece, pl.ds(0, NB), :],
            sem,
        )

    @pl.when(me == 0)
    def _():
        for piece in range(N_PROW):
            top_copy(piece).start()

    lax.fori_loop(0, NB, touch, 0)
    lax.fori_loop(0, NB, touch_top, 0)
    lax.fori_loop(0, NB, swap, 0)

    def send(j, extras):
        row = order[j]
        holder = holder_of(row)
        is_extra = jnp.logical_and(holder == 0, row >= NB)
        slot = jnp.where(holder == 0, jnp.where(row < NB, row, NB + extras), j)
        top_from[j] = holder * SEND_ROWS + slot

        @pl.when(jnp.logical_and(holder == me, row >= NB))
        def _():
            for piece in range(N_PROW):
                row_copy(local_of(row), slot, piece).start()

        return extras + jnp.where(is_extra, 1, 0)

    lax.fori_loop(0, NB, send, 0)

    def clear(q, carry):
        count[q] = 0
        return carry

    lax.fori_loop(0, N_PROW, clear, 0)

    def place(j, carry):
        row = pivots[j]
        outside = row >= NB
        q = jnp.where(outside, holder_of(row), 0)
        slot = count[q]
        count[q] = slot + jnp.where(outside, 1, 0)
        moved[2 * j] = jnp.where(outside, q * BACK_ROWS + NB + slot, -1)
        moved[2 * j + 1] = jnp.where(outside, order[row], 0)

        @pl.when(jnp.logical_and(outside, q == me))
        def _():
            own[1 + slot] = local_of(row)

        return carry

    lax.fori_loop(0, NB, place, 0)
    own[0] = count[me]

    @pl.when(me == 0)
    def _():
        for piece in range(N_PROW):
            top_copy(piece).wait()

    def finish(j, carry):
        row = order[j]

        @pl.when(jnp.logical_and(holder_of(row) == me, row >= NB))
        def _():
            for piece in range(N_PROW):
                row_copy(0, 0, piece).wait()

        return carry

    lax.fori_loop(0, NB, finish, 0)


def pick(pivots, trailing):
    return pl.pallas_call(
        pick_kernel,
        out_shape=(
            jax.ShapeDtypeStruct((N_PROW, SEND_ROWS, LANES), F32),
            jax.ShapeDtypeStruct((NB,), jnp.int32),
            jax.ShapeDtypeStruct((2 * NB,), jnp.int32),
            jax.ShapeDtypeStruct((2 * NB,), jnp.int32),
        ),
        in_specs=[pl.BlockSpec(memory_space=pltpu.SMEM), pl.BlockSpec(memory_space=pl.ANY)],
        out_specs=(
            pl.BlockSpec(memory_space=pltpu.VMEM),
            pl.BlockSpec(memory_space=pltpu.SMEM),
            pl.BlockSpec(memory_space=pltpu.SMEM),
            pl.BlockSpec(memory_space=pltpu.SMEM),
        ),
        scratch_shapes=[
            pltpu.SMEM((ROWS,), jnp.int32),
            pltpu.SMEM((N_PROW,), jnp.int32),
            pltpu.SemaphoreType.DMA,
        ],
        compiler_params=pltpu.CompilerParams(vmem_limit_bytes=32 * 2**20),
    )(pivots, trailing)


def spread_kernel(top_from, moved, got, diagonal, back):
    def gather(j, carry):
        back[pl.ds(j, 1), :] = got[pl.ds(top_from[j], 1), :]
        return carry

    lax.fori_loop(0, NB, gather, 0)
    half = NB // 2
    for q in range(N_PROW):
        base = q * BACK_ROWS
        if q > 0:
            back[base : base + NB, :] = back[0:NB, :]
        low = base + NB + DISPLACED
        back[low : low + half, 0:NB] = diagonal[0:half, 0:NB]
        back[low : low + half, NB:LANES] = diagonal[half:NB, 0:NB]

    def displace(j, carry):
        target = moved[2 * j]

        @pl.when(target >= 0)
        def _():
            back[pl.ds(target, 1), :] = got[pl.ds(moved[2 * j + 1], 1), :]

        return carry

    lax.fori_loop(0, NB, displace, 0)


def spread(top_from, moved, got, diagonal):
    return pl.pallas_call(
        spread_kernel,
        out_shape=jax.ShapeDtypeStruct((N_PROW * BACK_ROWS, LANES), F32),
        in_specs=[
            pl.BlockSpec(memory_space=pltpu.SMEM),
            pl.BlockSpec(memory_space=pltpu.SMEM),
            pl.BlockSpec(memory_space=pltpu.VMEM),
            pl.BlockSpec(memory_space=pltpu.VMEM),
        ],
        out_specs=pl.BlockSpec(memory_space=pltpu.VMEM),
        compiler_params=pltpu.CompilerParams(vmem_limit_bytes=32 * 2**20),
    )(top_from, moved, got, diagonal)


def halves(x):
    high = x.astype(BF16)
    return high, (x - high.astype(F32)).astype(BF16)


def thirds(x):
    high = x.astype(BF16)
    rest = x - high.astype(F32)
    mid = rest.astype(BF16)
    return high, mid, (rest - mid.astype(F32)).astype(BF16)


CHUNK = 512
N_CHUNK = 4


def update_kernel(
    own, given, panel, trailing, updated, block, multipliers, columns, arrive, leave
):
    me = lax.axis_index("prow")

    def load(k):
        cols = pl.ds(k * CHUNK, CHUNK)
        return pltpu.make_async_copy(trailing.at[:, cols], block.at[:, cols], arrive.at[k])

    def store(k):
        cols = pl.ds(k * CHUNK, CHUNK)
        return pltpu.make_async_copy(block.at[:, cols], updated.at[:, cols], leave.at[k])

    for k in range(N_CHUNK):
        load(k).start()

    for c in range(N_PCOL):
        high, low = halves(panel[c * NB : (c + 1) * NB, :].T)
        rows = slice(c * LANES, (c + 1) * LANES)
        multipliers[rows, :] = jnp.concatenate([high, low, high, low], axis=1)

    packed = given[NB + DISPLACED : BACK_ROWS, :]
    stacked = jnp.concatenate([packed[:, 0:NB], packed[:, NB:LANES]], axis=0)
    lower = stacked.T
    row_id = lax.broadcasted_iota(jnp.int32, (NB, NB), 0)
    col_id = lax.broadcasted_iota(jnp.int32, (NB, NB), 1)
    lower = jnp.where(col_id < row_id, lower, 0.0)
    for j in range(NB):
        columns[j] = jnp.broadcast_to(lower[:, j : j + 1], (NB, LANES))

    row_id = lax.broadcasted_iota(jnp.int32, (8, LANES), 0)
    col_id = lax.broadcasted_iota(jnp.int32, (8, LANES), 1)
    inverse = [jnp.where(col_id == row_id + 8 * b, 1.0, 0.0).astype(F32) for b in range(8)]
    for j in range(NB):
        b, s = j // 8, j % 8
        row = jnp.broadcast_to(inverse[b][s : s + 1, :], (8, LANES))
        for i in range(b, 8):
            inverse[i] = inverse[i] - columns[j, 8 * i : 8 * i + 8, :] * row
    inv_high, inv_mid, inv_low = thirds(jnp.concatenate(inverse, axis=0)[:, 0:NB])
    left = jnp.concatenate([inv_high, inv_mid, inv_low, inv_high, inv_mid, inv_high], axis=1)

    n_own = own[0]
    for k in range(N_CHUNK):
        cols = slice(k * CHUNK, (k + 1) * CHUNK)
        pieces = range(k * CHUNK // LANES, (k + 1) * CHUNK // LANES)
        swapped = jnp.concatenate(
            [given[p * BACK_ROWS : p * BACK_ROWS + NB, :] for p in pieces], axis=1
        )
        high, mid, low = thirds(swapped)
        right = jnp.concatenate([high, high, high, mid, mid, low], axis=0)
        upper = jnp.dot(left, right, preferred_element_type=F32)
        up_high, up_low = halves(upper)
        factor = jnp.concatenate([up_high, up_high, up_low, up_low], axis=0)
        load(k).wait()

        def displace(slot, carry):
            row = own[1 + slot]
            group = pl.ds(pl.multiple_of(row // 8 * 8, 8), 8)
            for p in pieces:
                source = given[pl.ds(p * BACK_ROWS + NB + slot, 1), :]
                part = slice(p * LANES, (p + 1) * LANES)
                block[group, part] = jnp.where(row_id == row % 8, source, block[group, part])
            return carry

        lax.fori_loop(0, n_own, displace, 0)
        product = jnp.dot(multipliers[...], factor, preferred_element_type=F32)
        block[:, cols] = block[:, cols] - product

        @pl.when(me == 0)
        def _():
            block[0:NB, cols] = upper

        store(k).start()
    for k in range(N_CHUNK):
        store(k).wait()


def update(own, given, panel, trailing):
    rows, cols = trailing.shape
    return pl.pallas_call(
        update_kernel,
        out_shape=jax.ShapeDtypeStruct((rows, cols), F32),
        in_specs=[
            pl.BlockSpec(memory_space=pltpu.SMEM),
            pl.BlockSpec(memory_space=pltpu.VMEM),
            pl.BlockSpec(memory_space=pltpu.VMEM),
            pl.BlockSpec(memory_space=pl.ANY),
        ],
        out_specs=pl.BlockSpec(memory_space=pl.ANY),
        scratch_shapes=[
            pltpu.VMEM((rows, cols), F32),
            pltpu.VMEM((rows, 4 * NB), BF16),
            pltpu.VMEM((NB, NB, LANES), F32),
            pltpu.SemaphoreType.DMA((N_CHUNK,)),
            pltpu.SemaphoreType.DMA((N_CHUNK,)),
        ],
        compiler_params=pltpu.CompilerParams(vmem_limit_bytes=48 * 2**20),
    )(own, given, panel, trailing)


def body(trailing, factors, pivots):
    sent, top_from, moved, own = pick(pivots, trailing)
    copies = jnp.broadcast_to(factors[None], (N_PCOL, NB, LANES))
    panel = lax.all_to_all(copies, "pcol", 0, 0)
    got = lax.all_to_all(sent, "prow", 0, 0)
    back = spread(top_from, moved, got.reshape(N_PROW * SEND_ROWS, LANES), panel[0])
    given = lax.all_to_all(back.reshape(N_PROW, BACK_ROWS, LANES), "prow", 0, 0)
    return update(
        own,
        given.reshape(N_PROW * BACK_ROWS, LANES),
        panel.reshape(N_PCOL * NB, LANES),
        trailing,
    )


def solution(mesh):
    return jax.shard_map(
        body,
        mesh=mesh,
        in_specs=(P("prow", "pcol"), P(None, ("prow", "pcol")), P()),
        out_specs=P("prow", "pcol"),
        check_vma=False,
    )
```

time: 148 us -> 76 us (0.51)
  blocking collectives: 82.2 us -> 22.4 us
  matrix products: 17.3 us -> 0 us
  Pallas kernels: 0 us -> 17 us
  waiting for transfers between devices: 2.36 us -> 18.5 us
  local copies, waits for them, and re-layouts: 21.2 us -> 5.51 us
  between operations: 13.6 us -> 0.05 us
  starting transfers between devices: 0.01 us -> 12.1 us
  other arithmetic: 11 us -> 0 us
    psum x1 -> x0, blocking collectives: 69.4 us -> none  [broadcast(): return lax.psum(kept, axis)]
    all_to_all x0 -> x1, blocking collectives: none -> 22.4 us  [body(): given = lax.all_to_all(back.reshape(N_PROW, BACK_ROWS, LANES), 'prow', 0, 0)]
    all_to_all x0 -> x2, waiting for transfers between devices: none -> 18.5 us  [the longest x1 18.5 us: body(): got = lax.all_to_all(sent, 'prow', 0, 0)]
    pallas_call x0 -> x3, Pallas kernels: none -> 17 us  [the longest x1 7.91 us: pick(): pl.pallas_call(pick_kernel, out_shape=(jax.ShapeDtypeStruct((N_PROW, SEND...]
    dot_general x9 -> x0, matrix products: 16.7 us -> none  [the longest x1 11.2 us: body(): lax.dot_general(lax.all_gather(factors, 'pcol', axis=1, tiled=True), uppe...]
    all_gather x1 -> x0, blocking collectives: 12.8 us -> none  [body(): lax.all_gather(factors, 'pcol', axis=1, tiled=True)]
    all_to_all x0 -> x2, starting transfers between devices: none -> 12.1 us  [the longest x1 6.67 us: body(): got = lax.all_to_all(sent, 'prow', 0, 0)]
    scatter x1 -> x0, local copies, waits for them, and re-layouts: 8.27 us -> none  [body(): swapped = trailing.at[target_rows].set(displaced, mode='drop')]
  transfers between devices with their start and end apart: 1 -> 2, of which waited for: 1 -> 1; matrix products, arithmetic and copies ran while one was open for 3% -> 0% of each run, Pallas kernels for 0% -> 10%
where the time goes in v1:
time: 76 us; the launch traced here: 75.5 us
  blocking collectives  22.4 us (29%)
  waiting for transfers between devices  18.5 us (24%)
  Pallas kernels  17 us (22%)
  starting transfers between devices  12.1 us (16%)
  local copies, waits for them, and re-layouts  5.51 us (7%)
    all_to_all x1, blocking collectives, body(): given = lax.all_to_all(back.reshape(N_PROW, BACK_ROWS, LANES), 'prow', 0, 0)  22.4 us
    all_to_all x1, waiting for transfers between devices, body(): got = lax.all_to_all(sent, 'prow', 0, 0)  18.5 us
    pallas_call x1, Pallas kernels, pick(): pl.pallas_call(pick_kernel, out_shape=(jax.ShapeDtypeStruct((N_PROW, SEND...  7.91 us
    pallas_call x1, Pallas kernels, update(): pl.pallas_call(update_kernel, out_shape=jax.ShapeDtypeStruct((rows, cols)...  7.08 us
    all_to_all x1, starting transfers between devices, body(): got = lax.all_to_all(sent, 'prow', 0, 0)  6.67 us
    all_to_all x1, starting transfers between devices, body(): panel = lax.all_to_all(copies, 'pcol', 0, 0)  5.4 us
    unnamed x4, local copies, waits for them, and re-layouts  4.03 us
    pallas_call x1, Pallas kernels, spread(): pl.pallas_call(spread_kernel, out_shape=jax.ShapeDtypeStruct((N_PROW * BA...  2.04 us
  transfers between devices with their start and end apart: 2, of which 1 were waited for; matrix products, arithmetic and copies ran while one was open for 0% of the time, Pallas kernels for 10%

profile of v1, /device:TPU:0, one launch (start us, length us, event | category | flops | bytes accessed | tf_op | source)
XLA Modules:
  0.0 75.5 jit_solution(2334683351911712613)
XLA Ops:
  0.0 1.5 %broadcast_in_dim.2 = f32[8,64,128]{2,1,0:T(8,128)} broadcast(f32[64,128]{1,0:T(8,128)} %param.4), dimensions={1,2} | broadcast | bytes 294912 | tf_op jit(solution)/shard_map/broadcast_in_dim | solution.py:317
  1.5 5.4 %all-to-all-start.1 = ((f32[8,64,128]{2,1,0:T(8,128)}), f32[8,64,128]{2,1,0:T(8,128)S(1)}, u32[]{:S(2)}, u32[]{:S(2)}) async-start(f32[8,64,128]{2,1,0:T(8,128)} %broadcast_in_dim.2), calls=%async_computation.1 | async-start | bytes 524288 | tf_op jit(solution)/shard_map/all_to_all | solution.py:318
  6.9 0.0 copy-start
  6.9 3.4 %copy-done = f32[1024,2048]{1,0:T(8,128)S(1)} copy-done((f32[1024,2048]{1,0:T(8,128)S(1)}, f32[1024,2048]{1,0:T(8,128)}, u32[]{:S(2)}) %copy-start) | copy-done | bytes 8388632
  10.3 0.0 copy-start.1
  10.3 0.7 copy-done.1
  10.9 7.9 %shard_map.37 = (f32[16,128,128]{2,1,0:T(8,128)}, s32[64]{0:T(128)S(1)}, s32[128]{0:T(128)S(1)}, s32[128]{0:T(128)S(1)}) custom-call(s32[64]{0:T(128)S(1)} %copy-done.1, f32[1024,2048]{1,0:T(8,128)S(1)} %copy-done), custom_call_target="tpu_custom_call" | custom-call | tf_op jit(solution)/shard_map/pallas_call | solution.py:133
  18.8 0.0 all-to-all-done.1
  18.8 6.7 %all-to-all-start = ((f32[16,128,128]{2,1,0:T(8,128)}), f32[16,128,128]{2,1,0:T(8,128)S(1)}, u32[]{:S(2)}, u32[]{:S(2)}) async-start(f32[16,128,128]{2,1,0:T(8,128)} %get-tuple-element.12), calls=%async_computation | async-start | bytes 2097152 | tf_op jit(solution)/shard_map/all_to_all | solution.py:319
  25.5 18.5 %all-to-all-done = f32[16,128,128]{2,1,0:T(8,128)S(1)} async-done(((f32[16,128,128]{2,1,0:T(8,128)}), f32[16,128,128]{2,1,0:T(8,128)S(1)}, u32[]{:S(2)}, u32[]{:S(2)}) %all-to-all-start) | async-done | bytes 1048608 | tf_op jit(solution)/shard_map/all_to_all | solution.py:319
  44.0 2.0 %shard_map.38 = f32[2560,128]{1,0:T(8,128)S(1)} custom-call(s32[64]{0:T(128)S(1)} %get-tuple-element.10.top_from, s32[128]{0:T(128)S(1)} %get-tuple-element.11.moved, f32[2048,128]{1,0:T(8,128)S(1)} %bitcast.8, f32[64,128]{1,0:T(8,128)S(1)} %slice_bitcast_fusion.diagonal), custom_call_target="tpu_custom_call" | custom-call | tf_op jit(solution)/shard_map/pallas_call | solution.py:185
  46.1 22.4 %all_to_all.15 = f32[16,160,128]{2,1,0:T(8,128)S(1)} all-to-all(f32[16,160,128]{2,1,0:T(8,128)S(1)} %bitcast.6), channel_id=1, replica_groups=mesh['prow'=16,'pcol'=8] {'prow'}, dimensions={0} | all-to-all | bytes 2621440 | tf_op jit(solution)/shard_map/all_to_all | solution.py:321
  68.4 7.1 %shard_map.39 = f32[1024,2048]{1,0:T(8,128)} custom-call(s32[128]{0:T(128)S(1)} %get-tuple-element.9.own, f32[2560,128]{1,0:T(8,128)S(1)} %bitcast.7, f32[512,128]{1,0:T(8,128)S(1)} %bitcast.9, f32[1024,2048]{1,0:T(8,128)} %trailing.3), custom_call_target="tpu_custom_call" | custom-call | tf_op jit(solution)/shard_map/pallas_call | solution.py:294
  (1 shorter events, 0.0 us)
Async XLA Ops:
  1.5 17.4 %all-to-all-start.1 = ((f32[8,64,128]{2,1,0:T(8,128)}), f32[8,64,128]{2,1,0:T(8,128)S(1)}, u32[]{:S(2)}, u32[]{:S(2)}) async-start(f32[8,64,128]{2,1,0:T(8,128)} %broadcast_in_dim.2), calls=%async_computation.1 | async-start | bytes 524288 | tf_op jit(solution)/shard_map/all_to_all | solution.py:318
  6.9 3.4 %copy-start = (f32[1024,2048]{1,0:T(8,128)S(1)}, f32[1024,2048]{1,0:T(8,128)}, u32[]{:S(2)}) copy-start(f32[1024,2048]{1,0:T(8,128)} %trailing.3) | copy-start | bytes 25165828
  10.3 0.7 copy-start.1
  18.8 25.2 %all-to-all-start = ((f32[16,128,128]{2,1,0:T(8,128)}), f32[16,128,128]{2,1,0:T(8,128)S(1)}, u32[]{:S(2)}, u32[]{:S(2)}) async-start(f32[16,128,128]{2,1,0:T(8,128)} %get-tuple-element.12), calls=%async_computation | async-start | bytes 2097152 | tf_op jit(solution)/shard_map/all_to_all | solution.py:319

commit v2 on v1

v2 whole, which is shorter than its diff:
```python
import functools

import jax
import jax.numpy as jnp
from jax import lax
from jax.experimental import pallas as pl
from jax.experimental.pallas import tpu as pltpu
from jax.sharding import PartitionSpec as P

LANES = 128
NB = 64
N_PROW = 16
N_PCOL = 8
ROWS = 16384
FEW = 16
LOWER = 16
F32 = jnp.float32
BF16 = jnp.bfloat16


def holder_of(row):
    return (row >> 6) & (N_PROW - 1)


def local_of(row):
    return ((row >> 10) << 6) | (row & (NB - 1))


def swap_chain(pivots, order, visit):
    for j in range(NB):
        order[pivots[j]] = pivots[j]
    for j in range(NB):
        order[j] = j
    for j in range(NB):
        k = pivots[j]
        row = order[k]
        order[k] = order[j]
        visit(j, row)


def swap_chain(pivots, order, visit):
    for j in range(NB):
        order[pivots[j]] = pivots[j]
    for j in range(NB):
        order[j] = j
    for j in range(NB):
        k = pivots[j]
        row = order[k]
        order[k] = order[j]
        visit(j, row)


def pick_kernel(pivots, trailing, sent, more, state, order, count, sem, top_sem):
    me = lax.axis_index("prow")

    def row_copy(row, slot, piece, target):
        return pltpu.make_async_copy(
            trailing.at[pl.ds(row, 1), pl.ds(piece * LANES, LANES)],
            target.at[piece, pl.ds(slot, 1), :],
            sem,
        )

    def top_copy(piece):
        return pltpu.make_async_copy(
            trailing.at[pl.ds(0, NB), pl.ds(piece * LANES, LANES)],
            sent.at[piece, pl.ds(0, NB), :],
            top_sem.at[piece],
        )

    @pl.when(me == 0)
    def _():
        for piece in range(N_PROW):
            top_copy(piece).start()

    count[N_PROW] = 0
    count[N_PROW + 1] = 0

    def visit(j, row):
        holder = holder_of(row)
        extra = count[N_PROW + 1]
        is_extra = jnp.logical_and(holder == 0, row >= NB)
        count[N_PROW + 1] = extra + jnp.where(is_extra, 1, 0)

        @pl.when(jnp.logical_and(holder == me, row >= NB))
        def _():
            count[N_PROW] = count[N_PROW] + 1
            slot = jnp.where(me == 0, NB + extra, j)
            local = local_of(row)

            @pl.when(slot < NB + FEW)
            def _():
                for piece in range(N_PROW):
                    row_copy(local, slot, piece, sent).start()

            @pl.when(slot >= NB + FEW)
            def _():
                for piece in range(N_PROW):
                    row_copy(local, slot - (NB + FEW), piece, more).start()

    swap_chain(pivots, order, visit)
    for q in range(N_PROW):
        count[q] = 0
    for j in range(NB):
        row = pivots[j]
        q = holder_of(row)
        count[q] = count[q] + jnp.where(row >= NB, 1, 0)
    most = count[N_PROW + 1]
    for q in range(N_PROW):
        most = jnp.maximum(most, count[q])
    state[0] = me
    state[1] = jnp.where(most > FEW, 1, 0)

    @pl.when(me == 0)
    def _():
        for piece in range(N_PROW):
            top_copy(piece).wait()

    def finish(i, carry):
        for piece in range(N_PROW):
            row_copy(0, 0, piece, sent).wait()
        return carry

    lax.fori_loop(0, count[N_PROW], finish, 0)


def pick(pivots, trailing):
    return pl.pallas_call(
        pick_kernel,
        out_shape=(
            jax.ShapeDtypeStruct((N_PROW, NB + FEW, LANES), F32),
            jax.ShapeDtypeStruct((N_PROW, NB - FEW, LANES), F32),
            jax.ShapeDtypeStruct((2,), jnp.int32),
        ),
        in_specs=[
            pl.BlockSpec(memory_space=pltpu.SMEM),
            pl.BlockSpec(memory_space=pltpu.HBM),
        ],
        out_specs=(
            pl.BlockSpec(memory_space=pltpu.VMEM),
            pl.BlockSpec(memory_space=pltpu.VMEM),
            pl.BlockSpec(memory_space=pltpu.SMEM),
        ),
        scratch_shapes=[
            pltpu.SMEM((ROWS,), jnp.int32),
            pltpu.SMEM((N_PROW + 2,), jnp.int32),
            pltpu.SemaphoreType.DMA,
            pltpu.SemaphoreType.DMA((N_PROW,)),
        ],
        compiler_params=pltpu.CompilerParams(vmem_limit_bytes=58 * 2**20),
    )(pivots, trailing)


TOP_FROM = 0
MOVED = NB
OWN = 3 * NB
TABLE = 5 * NB


def route_kernel(room, pivots, state, mine, other, table, pair, order, count):
    send_rows, back_rows = NB + room, NB + room + LOWER
    me = state[0]
    pair[0:NB, :] = mine[...]
    pair[NB : 2 * NB, :] = other[...]
    count[N_PROW] = 0

    def visit(j, row):
        holder = holder_of(row)
        extra = count[N_PROW]
        count[N_PROW] = extra + jnp.where(jnp.logical_and(holder == 0, row >= NB), 1, 0)
        slot = jnp.where(holder == 0, jnp.where(row < NB, row, NB + extra), j)
        table[TOP_FROM + j] = holder * send_rows + slot

    swap_chain(pivots, order, visit)
    for q in range(N_PROW):
        count[q] = 0
    for j in range(NB):
        row = pivots[j]
        outside = row >= NB
        q = jnp.where(outside, holder_of(row), 0)
        slot = count[q]
        count[q] = slot + jnp.where(outside, 1, 0)
        table[MOVED + 2 * j] = jnp.where(outside, q * back_rows + NB + slot, -1)
        table[MOVED + 2 * j + 1] = jnp.where(outside, order[row], 0)

        @pl.when(jnp.logical_and(outside, q == me))
        def _():
            table[OWN + 1 + slot] = local_of(row)

    table[OWN] = count[me]


def route(room, pivots, state, mine, other):
    smem = pl.BlockSpec(memory_space=pltpu.SMEM)
    vmem = pl.BlockSpec(memory_space=pltpu.VMEM)
    return pl.pallas_call(
        functools.partial(route_kernel, room),
        out_shape=(
            jax.ShapeDtypeStruct((TABLE,), jnp.int32),
            jax.ShapeDtypeStruct((2 * NB, LANES), F32),
        ),
        in_specs=[smem, smem, vmem, vmem],
        out_specs=(smem, vmem),
        scratch_shapes=[
            pltpu.SMEM((ROWS,), jnp.int32),
            pltpu.SMEM((N_PROW + 1,), jnp.int32),
        ],
    )(pivots, state, mine, other)


HALF = NB // 2


def fold(diagonal):
    row_id = lax.broadcasted_iota(jnp.int32, (HALF, HALF), 0)
    col_id = lax.broadcasted_iota(jnp.int32, (HALF, HALF), 1)
    first = diagonal[0:HALF, 0:HALF]
    last = diagonal[HALF:NB, HALF:NB]
    mixed = jnp.where(col_id > row_id, first, last.T)
    both = jnp.concatenate([mixed, diagonal[0:HALF, HALF:NB]], axis=1)
    return jnp.concatenate([both[0:LOWER], both[LOWER:HALF]], axis=1)


def unfold(packed):
    row_id = lax.broadcasted_iota(jnp.int32, (HALF, HALF), 0)
    col_id = lax.broadcasted_iota(jnp.int32, (HALF, HALF), 1)
    both = jnp.concatenate([packed[:, 0:NB], packed[:, NB:LANES]], axis=0)
    mixed = both[:, 0:HALF]
    zero = jnp.zeros((HALF, HALF), F32)
    first = jnp.where(col_id < row_id, mixed.T, zero)
    last = jnp.where(col_id < row_id, mixed, zero)
    top = jnp.concatenate([first, zero], axis=1)
    return jnp.concatenate([top, jnp.concatenate([both[:, HALF:NB].T, last], axis=1)], axis=0)


def spread_kernel(room, table, got, here, below, above, across, back, diagonal):
    back_rows = NB + room + LOWER
    c = lax.axis_index("pcol")
    z, core = c // 2, c % 2
    for place, pair in enumerate((here, below, across, above)):

        @pl.when(z == place)
        def _():
            start = pl.multiple_of(core * NB, NB)
            diagonal[...] = pair[pl.ds(start, NB), :]

    for j in range(NB):
        back[j : j + 1, :] = got[pl.ds(table[TOP_FROM + j], 1), :]
    packed = fold(diagonal[:, 0:NB])
    for q in range(N_PROW):
        base = q * back_rows
        if q > 0:
            back[base : base + NB, :] = back[0:NB, :]
        low = base + NB + room
        back[low : low + LOWER, :] = packed

    for j in range(NB):
        target = table[MOVED + 2 * j]

        @pl.when(target >= 0)
        def _():
            back[pl.ds(target, 1), :] = got[pl.ds(table[MOVED + 2 * j + 1], 1), :]


def spread(room, table, got, pairs):
    vmem = pl.BlockSpec(memory_space=pltpu.VMEM)
    back_rows = NB + room + LOWER
    return pl.pallas_call(
        functools.partial(spread_kernel, room),
        out_shape=jax.ShapeDtypeStruct((N_PROW * back_rows, LANES), F32),
        in_specs=[pl.BlockSpec(memory_space=pltpu.SMEM)] + [vmem] * 5,
        out_specs=vmem,
        scratch_shapes=[pltpu.VMEM((NB, LANES), F32)],
        compiler_params=pltpu.CompilerParams(vmem_limit_bytes=32 * 2**20),
    )(table, got, *pairs)


def halves(x):
    high = x.astype(BF16)
    return high, (x - high.astype(F32)).astype(BF16)


def thirds(x):
    high = x.astype(BF16)
    rest = x - high.astype(F32)
    mid = rest.astype(BF16)
    return high, mid, (rest - mid.astype(F32)).astype(BF16)


CHUNK = 512
N_CHUNK = 4


def update_kernel(
    room,
    table,
    given,
    here,
    below,
    above,
    across,
    trailing,
    updated,
    block,
    multipliers,
    columns,
    arrive,
    leave,
):
    back_rows = NB + room + LOWER
    me = lax.axis_index("prow")
    c = lax.axis_index("pcol")
    z, core = c // 2, c % 2

    def load(k):
        cols = pl.ds(k * CHUNK, CHUNK)
        return pltpu.make_async_copy(trailing.at[:, cols], block.at[:, cols], arrive.at[k])

    def store(k):
        cols = pl.ds(k * CHUNK, CHUNK)
        return pltpu.make_async_copy(block.at[:, cols], updated.at[:, cols], leave.at[k])

    for k in range(N_CHUNK):
        load(k).start()

    for step, pair in ((0, here), (3, below), (1, above), (2, across)):
        for side in range(2):
            high, low = halves(pair[side * NB : (side + 1) * NB, :].T)
            place = ((z + step) % 4) * 2 + (core + side) % 2
            start = pl.multiple_of(place * LANES, LANES)
            multipliers[pl.ds(start, LANES), :] = jnp.concatenate([high, low, high, low], axis=1)

    lower = unfold(given[NB + room : back_rows, :])
    for j in range(NB):
        columns[j] = jnp.broadcast_to(lower[:, j : j + 1], (NB, LANES))

    row_id = lax.broadcasted_iota(jnp.int32, (8, LANES), 0)
    col_id = lax.broadcasted_iota(jnp.int32, (8, LANES), 1)
    inverse = [jnp.where(col_id == row_id + 8 * b, 1.0, 0.0).astype(F32) for b in range(8)]
    for j in range(NB):
        b, s = j // 8, j % 8
        row = jnp.broadcast_to(inverse[b][s : s + 1, :], (8, LANES))
        for i in range(b, 8):
            inverse[i] = inverse[i] - columns[j, 8 * i : 8 * i + 8, :] * row
    inv_high, inv_mid, inv_low = thirds(jnp.concatenate(inverse, axis=0)[:, 0:NB])
    left = jnp.concatenate([inv_high, inv_mid, inv_low, inv_high, inv_mid, inv_high], axis=1)

    n_own = table[OWN]
    for k in range(N_CHUNK):
        cols = slice(k * CHUNK, (k + 1) * CHUNK)
        pieces = range(k * CHUNK // LANES, (k + 1) * CHUNK // LANES)
        swapped = jnp.concatenate(
            [given[p * back_rows : p * back_rows + NB, :] for p in pieces], axis=1
        )
        high, mid, low = thirds(swapped)
        right = jnp.concatenate([high, high, high, mid, mid, low], axis=0)
        upper = jnp.dot(left, right, preferred_element_type=F32)
        up_high, up_low = halves(upper)
        factor = jnp.concatenate([up_high, up_high, up_low, up_low], axis=0)
        load(k).wait()

        def displace(slot, carry):
            row = table[OWN + 1 + slot]
            group = pl.ds(pl.multiple_of(row // 8 * 8, 8), 8)
            for p in pieces:
                source = given[pl.ds(p * back_rows + NB + slot, 1), :]
                part = slice(p * LANES, (p + 1) * LANES)
                block[group, part] = jnp.where(row_id == row % 8, source, block[group, part])
            return carry

        lax.fori_loop(0, n_own, displace, 0)
        product = jnp.dot(multipliers[...], factor, preferred_element_type=F32)
        block[:, cols] = block[:, cols] - product

        @pl.when(me == 0)
        def _():
            block[0:NB, cols] = upper

        store(k).start()
    for k in range(N_CHUNK):
        store(k).wait()


def update(room, table, given, pairs, trailing):
    rows, cols = trailing.shape
    vmem = pl.BlockSpec(memory_space=pltpu.VMEM)
    return pl.pallas_call(
        functools.partial(update_kernel, room),
        out_shape=jax.ShapeDtypeStruct((rows, cols), F32),
        in_specs=[pl.BlockSpec(memory_space=pltpu.SMEM)]
        + [vmem] * 5
        + [pl.BlockSpec(memory_space=pltpu.HBM)],
        out_specs=pl.BlockSpec(memory_space=pltpu.HBM),
        scratch_shapes=[
            pltpu.VMEM((rows, cols), F32),
            pltpu.VMEM((rows, 4 * NB), BF16),
            pltpu.VMEM((NB, NB, LANES), F32),
            pltpu.SemaphoreType.DMA((N_CHUNK,)),
            pltpu.SemaphoreType.DMA((N_CHUNK,)),
        ],
        compiler_params=pltpu.CompilerParams(vmem_limit_bytes=58 * 2**20),
    )(table, given, *pairs, trailing)


def ring(step):
    return [(c, (c // 2 + step) % 4 * 2 + c % 2) for c in range(N_PCOL)]


def rest(room, trailing, factors, partner, pivots, sent, state):
    got = lax.all_to_all(sent, "prow", 0, 0)
    table, pair = route(room, pivots, state, factors, partner)
    below = lax.ppermute(pair, "pcol", ring(1))
    above = lax.ppermute(pair, "pcol", ring(3))
    across = lax.ppermute(pair, "pcol", ring(2))
    pairs = (pair, below, above, across)
    back = spread(room, table, got.reshape(-1, LANES), pairs)
    given = lax.all_to_all(back.reshape(N_PROW, -1, LANES), "prow", 0, 0)
    return update(room, table, given.reshape(-1, LANES), pairs, trailing)


def body(trailing, factors, pivots):
    partner = lax.ppermute(factors, "pcol", [(c, c ^ 1) for c in range(N_PCOL)])
    sent, more, state = pick(pivots, trailing)

    def few(sent, more):
        return rest(FEW, trailing, factors, partner, pivots, sent, state)

    def many(sent, more):
        every = jnp.concatenate([sent, more], axis=1)
        return rest(NB, trailing, factors, partner, pivots, every, state)

    return lax.cond(state[1] == 0, few, many, sent, more)


def solution(mesh):
    return jax.shard_map(
        body,
        mesh=mesh,
        in_specs=(P("prow", "pcol"), P(None, ("prow", "pcol")), P()),
        out_specs=P("prow", "pcol"),
        check_vma=False,
    )
```

time: 76 us -> 56.5 us (0.74)
  waiting for transfers between devices: 18.5 us -> 5.41 us
  blocking collectives: 22.4 us -> 18.5 us
  local copies, waits for them, and re-layouts: 5.51 us -> 2.09 us
  Pallas kernels: 17 us -> 15.7 us
  starting transfers between devices: 12.1 us -> 13.3 us
  between operations: 0.05 us -> 0.87 us
    all_to_all x2 -> x1, waiting for transfers between devices: 18.5 us -> 1.04 us  [rest(): got = lax.all_to_all(sent, 'prow', 0, 0)]
    ppermute x0 -> x4, starting transfers between devices: none -> 5.98 us  [the longest x1 3.96 us: rest(): across = lax.ppermute(pair, 'pcol', ring(2))]
    all_to_all x2 -> x1, starting transfers between devices: 12.1 us -> 7.28 us  [rest(): got = lax.all_to_all(sent, 'prow', 0, 0)]
    ppermute x0 -> x4, waiting for transfers between devices: none -> 4.37 us  [the longest x1 2.16 us: rest(): above = lax.ppermute(pair, 'pcol', ring(3))]
    unnamed x4, local copies, waits for them, and re-layouts: 4.03 us -> 0.01 us
    all_to_all x1, blocking collectives: 22.4 us -> 18.5 us  [rest(): given = lax.all_to_all(back.reshape(N_PROW, -1, LANES), 'prow', 0, 0)]
    cond x0 -> x10, local copies, waits for them, and re-layouts: none -> 1.51 us
    broadcast_in_dim x1 -> x0, local copies, waits for them, and re-layouts: 1.48 us -> none  [body(): copies = jnp.broadcast_to(factors[None], (N_PCOL, NB, LANES))]
  transfers between devices with their start and end apart: 2 -> 5, of which waited for: 1 -> 4; matrix products, arithmetic and copies ran while one was open for 0% -> 1% of each run, Pallas kernels for 10% -> 10%
where the time goes in v2:
time: 56.5 us; the launch traced here: 56.1 us
  blocking collectives  18.5 us (33%)
  Pallas kernels  15.7 us (28%)
  starting transfers between devices  13.3 us (24%)
  waiting for transfers between devices  5.41 us (10%)
  local copies, waits for them, and re-layouts  2.09 us (4%)
  between operations  0.87 us (2%)
    all_to_all x1, blocking collectives, rest(): given = lax.all_to_all(back.reshape(N_PROW, -1, LANES), 'prow', 0, 0)  18.5 us
    pallas_call x1, Pallas kernels, update(): pl.pallas_call(functools.partial(update_kernel, room), out_shape=jax.Shap...  8.61 us
    all_to_all x1, starting transfers between devices, rest(): got = lax.all_to_all(sent, 'prow', 0, 0)  7.28 us
    ppermute x1, starting transfers between devices, rest(): across = lax.ppermute(pair, 'pcol', ring(2))  3.96 us
    pallas_call x1, Pallas kernels, pick(): pl.pallas_call(pick_kernel, out_shape=(jax.ShapeDtypeStruct((N_PROW, NB +...  3.65 us
    ppermute x1, waiting for transfers between devices, rest(): above = lax.ppermute(pair, 'pcol', ring(3))  2.16 us
    pallas_call x1, Pallas kernels, route(): pl.pallas_call(functools.partial(route_kernel, room), out_shape=(jax.Shap...  2.09 us
    ppermute x1, waiting for transfers between devices, rest(): below = lax.ppermute(pair, 'pcol', ring(1))  1.69 us
  transfers between devices with their start and end apart: 5, of which 4 were waited for; matrix products, arithmetic and copies ran while one was open for 1% of the time, Pallas kernels for 10%

profile of v2, /device:TPU:0, one launch (start us, length us, event | category | flops | bytes accessed | tf_op | source)
XLA Modules:
  0.0 56.1 jit_solution(16468060041085639567)
XLA Ops:
  0.0 0.0 copy-start.10
  0.0 0.0 copy-start.11
  0.0 0.0 collective-permute-start.6
  0.0 3.6 %shard_map.39 = (f32[16,80,128]{2,1,0:T(8,128)}, f32[16,48,128]{2,1,0:T(8,128)S(1)}, s32[2]{0:T(128)S(1)}) custom-call(s32[64]{0:T(128)} %pivots.1, f32[1024,2048]{1,0:T(8,128)} %trailing.1), custom_call_target="tpu_custom_call" | custom-call | tf_op jit(solution)/shard_map/pallas_call | solution.py:127
  3.7 0.6 %slice.3 = s32[1]{0:T(128)} slice(s32[2]{0:T(128)S(1)} %get-tuple-element.54), slice={[1:2]} | slice | bytes 8 | tf_op jit(solution)/shard_map/slice | solution.py:431
  4.9 0.0 collective-permute-done.6
  4.9 0.0 copy-done.10
  4.9 0.0 copy-done.11
  4.9 51.0 %conditional.1 = (f32[1024,2048]{1,0:T(8,128)}) conditional(s32[]{:T(128)} %bitcast.6, (s32[64]{0:T(128)S(1)}, s32[2]{0:T(128)S(1)}, f32[64,128]{1,0:T(8,128)S(1)}, f32[64,128]{1,0:T(8,128)S(1)}, f32[16,80,128]{2,1,0:T(8,128)}, /*index=5*/f32[16,48,128]{2,1,0:T(8,128)S(1)}, f32[1024,2048]{1,0:T(8,128)}) %tuple.19, (s32[64]{0:T(128)S(1)}, ...), branch_computations={%region_0.0_spmd, %region_1.0_spmd} | conditional | flops 262144 | bytes 9442604 | solution.py:431
  4.9 7.3 %all-to-all-start = ((f32[16,80,128]{2,1,0:T(8,128)}), f32[16,80,128]{2,1,0:T(8,128)S(1)}, u32[]{:S(2)}, u32[]{:S(2)}) async-start(f32[16,80,128]{2,1,0:T(8,128)} %get-tuple-element.48), calls=%async_computation | async-start | bytes 1310720 | tf_op jit(solution)/shard_map/cond/branch_1_fun/all_to_all | solution.py:409
  12.2 2.1 %branch_1_fun.3 = (s32[320]{0:T(512)}, f32[128,128]{1,0:T(8,128)}) custom-call(s32[64]{0:T(128)S(1)} %get-tuple-element.43.pivots, s32[2]{0:T(128)S(1)} %get-tuple-element.44.state, f32[64,128]{1,0:T(8,128)S(1)} %get-tuple-element.45.mine, f32[64,128]{1,0:T(8,128)S(1)} %get-tuple-element.46.other), custom_call_target="tpu_custom_call" | custom-call | tf_op jit(solution)/shard_map/cond/branch_1_fun/pallas_call | solution.py:195
  14.3 4.0 %collective-permute-start.2 = (f32[128,128]{1,0:T(8,128)}, f32[128,128]{1,0:T(8,128)S(1)}, u32[]{:S(2)}, u32[]{:S(2)}) collective-permute-start(f32[128,128]{1,0:T(8,128)} %get-tuple-element.49.here), channel_id=1, source_target_pairs={{0,4},{1,5},{2,6},{3,7},{4,0},{5,1},{6,2},{7,3},{8,12},{9,13},{10,... | collective-permute-start | bytes 196616 | tf_op jit(solution)/shard_map/cond/branch_1_fun/ppermute | solution.py:413
  18.3 0.7 %collective-permute-start.1 = (f32[128,128]{1,0:T(8,128)}, f32[128,128]{1,0:T(8,128)S(1)}, u32[]{:S(2)}, u32[]{:S(2)}) collective-permute-start(f32[128,128]{1,0:T(8,128)} %get-tuple-element.49.here), channel_id=1, source_target_pairs={{0,6},{1,7},{2,0},{3,1},{4,2},{5,3},{6,4},{7,5},{8,14},{9,15},{10,... | collective-permute-start | bytes 196616 | tf_op jit(solution)/shard_map/cond/branch_1_fun/ppermute | solution.py:412
  19.0 1.3 %collective-permute-start = (f32[128,128]{1,0:T(8,128)}, f32[128,128]{1,0:T(8,128)S(1)}, u32[]{:S(2)}, u32[]{:S(2)}) collective-permute-start(f32[128,128]{1,0:T(8,128)} %get-tuple-element.49.here), channel_id=1, source_target_pairs={{0,2},{1,3},{2,4},{3,5},{4,6},{5,7},{6,0},{7,1},{8,10},{9,11},{10,... | collective-permute-start | bytes 196616 | tf_op jit(solution)/shard_map/cond/branch_1_fun/ppermute | solution.py:411
  20.3 0.5 collective-permute-done.2.across
  20.8 0.0 copy-start.5
  20.8 2.2 %collective-permute-done.1.above = f32[128,128]{1,0:T(8,128)S(1)} collective-permute-done((f32[128,128]{1,0:T(8,128)}, f32[128,128]{1,0:T(8,128)S(1)}, u32[]{:S(2)}, u32[]{:S(2)}) %collective-permute-start.1) | collective-permute-done | bytes 65568 | tf_op jit(solution)/shard_map/cond/branch_1_fun/ppermute | solution.py:412
  23.0 0.0 copy-start.6
  23.0 1.7 %collective-permute-done.below = f32[128,128]{1,0:T(8,128)S(1)} collective-permute-done((f32[128,128]{1,0:T(8,128)}, f32[128,128]{1,0:T(8,128)S(1)}, u32[]{:S(2)}, u32[]{:S(2)}) %collective-permute-start) | collective-permute-done | bytes 65568 | tf_op jit(solution)/shard_map/cond/branch_1_fun/ppermute | solution.py:411
  24.7 0.0 copy-start.7
  24.7 1.0 %all-to-all-done = f32[16,80,128]{2,1,0:T(8,128)S(1)} async-done(((f32[16,80,128]{2,1,0:T(8,128)}), f32[16,80,128]{2,1,0:T(8,128)S(1)}, u32[]{:S(2)}, u32[]{:S(2)}) %all-to-all-start) | async-done | bytes 655392 | tf_op jit(solution)/shard_map/cond/branch_1_fun/all_to_all | solution.py:409
  25.7 0.0 copy-start.4
  25.7 0.8 %copy-done.4 = f32[128,128]{1,0:T(8,128)S(1)} copy-done((f32[128,128]{1,0:T(8,128)S(1)}, f32[128,128]{1,0:T(8,128)}, u32[]{:S(2)}) %copy-start.4) | copy-done | bytes 65560 | tf_op jit(solution)/shard_map/cond
  26.6 0.0 copy-start.8
  26.6 0.7 %copy-done.8 = s32[320]{0:T(512)S(1)} copy-done((s32[320]{0:T(512)S(1)}, s32[320]{0:T(512)}, u32[]{:S(2)}) %copy-start.8) | copy-done | bytes 1304 | tf_op jit(solution)/shard_map/cond
  27.2 1.4 %branch_1_fun.4 = f32[1536,128]{1,0:T(8,128)S(1)} custom-call(s32[320]{0:T(512)S(1)} %copy-done.8, f32[1280,128]{1,0:T(8,128)S(1)} %bitcast.10, f32[128,128]{1,0:T(8,128)S(1)} %copy-done.4, f32[128,128]{1,0:T(8,128)S(1)} %collective-permute-done.below, f32[128,128]{1,0:T(8,128)S(1)} %collective-permute-done.1.above, f32[128,128]{1,0:T(8,128)S(1)} %collective-permute-done.2.across), custom_call_target="tpu_custom_call" | custom-call | tf_op jit(solution)/shard_map/cond/branch_1_fun/pallas_call | solution.py:267
  28.6 18.5 %all_to_all.17 = f32[16,96,128]{2,1,0:T(8,128)} all-to-all(f32[16,96,128]{2,1,0:T(8,128)S(1)} %bitcast.9), channel_id=1, replica_groups=mesh['prow'=16,'pcol'=8] {'prow'}, dimensions={0} | all-to-all | bytes 1572864 | tf_op jit(solution)/shard_map/cond/branch_1_fun/all_to_all | solution.py:416
  47.1 0.0 copy-done.5
  47.1 0.0 copy-done.6
  47.1 0.0 copy-done.7
  47.1 8.6 %branch_1_fun.5 = f32[1024,2048]{1,0:T(8,128)} custom-call(s32[320]{0:T(512)} %get-tuple-element.47.table, f32[1536,128]{1,0:T(8,128)} %bitcast.12, f32[128,128]{1,0:T(8,128)} %get-tuple-element.49.here, f32[128,128]{1,0:T(8,128)} %copy-done.7, f32[128,128]{1,0:T(8,128)} %copy-done.6, f32[128,128]{1,0:T(8,128)} %copy-done.5, ...), custom_call_target="tpu_custom_call" | custom-call | tf_op jit(solution)/shard_map/cond/branch_1_fun/pallas_call | solution.py:386
Async XLA Ops:
  0.0 4.9 %copy-start.10 = (f32[64,128]{1,0:T(8,128)S(1)}, f32[64,128]{1,0:T(8,128)}, u32[]{:S(2)}) copy-start(f32[64,128]{1,0:T(8,128)} %param.6) | copy-start | bytes 98308
  0.0 4.9 %copy-start.11 = (s32[64]{0:T(128)S(1)}, s32[64]{0:T(128)}, u32[]{:S(2)}) copy-start(s32[64]{0:T(128)} %pivots.1) | copy-start | bytes 772
  0.0 4.9 %collective-permute-start.6 = (f32[64,128]{1,0:T(8,128)}, f32[64,128]{1,0:T(8,128)S(1)}, u32[]{:S(2)}, u32[]{:S(2)}) collective-permute-start(f32[64,128]{1,0:T(8,128)} %param.6), channel_id=1, source_target_pairs={{0,1},{1,0},{2,3},{3,2},{4,5},{5,4},{6,7},{7,6},{8,9},{9,8},{10,11... | collective-permute-start | bytes 98312 | tf_op jit(solution)/shard_map/ppermute | solution.py:421
  4.9 20.8 %all-to-all-start = ((f32[16,80,128]{2,1,0:T(8,128)}), f32[16,80,128]{2,1,0:T(8,128)S(1)}, u32[]{:S(2)}, u32[]{:S(2)}) async-start(f32[16,80,128]{2,1,0:T(8,128)} %get-tuple-element.48), calls=%async_computation | async-start | bytes 1310720 | tf_op jit(solution)/shard_map/cond/branch_1_fun/all_to_all | solution.py:409
  14.3 6.5 %collective-permute-start.2 = (f32[128,128]{1,0:T(8,128)}, f32[128,128]{1,0:T(8,128)S(1)}, u32[]{:S(2)}, u32[]{:S(2)}) collective-permute-start(f32[128,128]{1,0:T(8,128)} %get-tuple-element.49.here), channel_id=1, source_target_pairs={{0,4},{1,5},{2,6},{3,7},{4,0},{5,1},{6,2},{7,3},{8,12},{9,13},{10,... | collective-permute-start | bytes 196616 | tf_op jit(solution)/shard_map/cond/branch_1_fun/ppermute | solution.py:413
  18.3 4.7 %collective-permute-start.1 = (f32[128,128]{1,0:T(8,128)}, f32[128,128]{1,0:T(8,128)S(1)}, u32[]{:S(2)}, u32[]{:S(2)}) collective-permute-start(f32[128,128]{1,0:T(8,128)} %get-tuple-element.49.here), channel_id=1, source_target_pairs={{0,6},{1,7},{2,0},{3,1},{4,2},{5,3},{6,4},{7,5},{8,14},{9,15},{10,... | collective-permute-start | bytes 196616 | tf_op jit(solution)/shard_map/cond/branch_1_fun/ppermute | solution.py:412
  19.0 5.7 %collective-permute-start = (f32[128,128]{1,0:T(8,128)}, f32[128,128]{1,0:T(8,128)S(1)}, u32[]{:S(2)}, u32[]{:S(2)}) collective-permute-start(f32[128,128]{1,0:T(8,128)} %get-tuple-element.49.here), channel_id=1, source_target_pairs={{0,2},{1,3},{2,4},{3,5},{4,6},{5,7},{6,0},{7,1},{8,10},{9,11},{10,... | collective-permute-start | bytes 196616 | tf_op jit(solution)/shard_map/cond/branch_1_fun/ppermute | solution.py:411
  20.8 26.2 %copy-start.5 = (f32[128,128]{1,0:T(8,128)}, f32[128,128]{1,0:T(8,128)S(1)}, u32[]{:S(2)}) copy-start(f32[128,128]{1,0:T(8,128)S(1)} %collective-permute-done.2.across) | copy-start | bytes 196612 | tf_op jit(solution)/shard_map/cond
  23.0 24.1 %copy-start.6 = (f32[128,128]{1,0:T(8,128)}, f32[128,128]{1,0:T(8,128)S(1)}, u32[]{:S(2)}) copy-start(f32[128,128]{1,0:T(8,128)S(1)} %collective-permute-done.1.above) | copy-start | bytes 196612 | tf_op jit(solution)/shard_map/cond
  24.7 22.4 %copy-start.7 = (f32[128,128]{1,0:T(8,128)}, f32[128,128]{1,0:T(8,128)S(1)}, u32[]{:S(2)}) copy-start(f32[128,128]{1,0:T(8,128)S(1)} %collective-permute-done.below) | copy-start | bytes 196612 | tf_op jit(solution)/shard_map/cond
  25.7 0.8 %copy-start.4 = (f32[128,128]{1,0:T(8,128)S(1)}, f32[128,128]{1,0:T(8,128)}, u32[]{:S(2)}) copy-start(f32[128,128]{1,0:T(8,128)} %get-tuple-element.49.here) | copy-start | bytes 196612 | tf_op jit(solution)/shard_map/cond
  26.6 0.7 %copy-start.8 = (s32[320]{0:T(512)S(1)}, s32[320]{0:T(512)}, u32[]{:S(2)}) copy-start(s32[320]{0:T(512)} %get-tuple-element.47.table) | copy-start | bytes 3844 | tf_op jit(solution)/shard_map/cond

commit v3 on v2

v3 whole, which is shorter than its diff:
```python
import functools

import jax
import jax.numpy as jnp
from jax import lax
from jax.experimental import pallas as pl
from jax.experimental.pallas import tpu as pltpu
from jax.sharding import PartitionSpec as P

LANES = 128
NB = 64
N_PROW = 16
N_PCOL = 8
ROWS = 16384
FEW = 16
LOWER = 16
F32 = jnp.float32
BF16 = jnp.bfloat16


def holder_of(row):
    return (row >> 6) & (N_PROW - 1)


def local_of(row):
    return ((row >> 10) << 6) | (row & (NB - 1))


def swap_chain(pivots, order, visit):
    for j in range(NB):
        order[pivots[j]] = pivots[j]
    for j in range(NB):
        order[j] = j
    for j in range(NB):
        k = pivots[j]
        row = order[k]
        order[k] = order[j]
        visit(j, row)


def pick_kernel(room, pivots, trailing, sent, order, count, mine, sem, top_sem):
    me = lax.axis_index("prow")

    def row_copy(row, slot, piece):
        return pltpu.make_async_copy(
            trailing.at[pl.ds(row, 1), pl.ds(piece * LANES, LANES)],
            sent.at[piece, pl.ds(slot, 1), :],
            sem,
        )

    def top_copy(piece):
        return pltpu.make_async_copy(
            trailing.at[pl.ds(0, NB), pl.ds(piece * LANES, LANES)],
            sent.at[piece, pl.ds(0, NB), :],
            top_sem.at[piece],
        )

    @pl.when(me == 0)
    def _():
        for piece in range(N_PROW):
            top_copy(piece).start()

    count[0] = 0

    def visit(j, row):
        place = count[0]
        mine[2 * place] = local_of(row)
        mine[2 * place + 1] = jnp.where(me == 0, NB + place, j)
        wanted = jnp.logical_and(holder_of(row) == me, row >= NB)
        count[0] = place + jnp.where(wanted, 1, 0)

    swap_chain(pivots, order, visit)
    n_mine = jnp.where(me == 0, jnp.minimum(count[0], room), count[0])

    def send(i, carry):
        for piece in range(N_PROW):
            row_copy(mine[2 * i], mine[2 * i + 1], piece).start()
        return carry

    lax.fori_loop(0, n_mine, send, 0)

    @pl.when(me == 0)
    def _():
        for piece in range(N_PROW):
            top_copy(piece).wait()

    def finish(i, carry):
        for piece in range(N_PROW):
            row_copy(0, 0, piece).wait()
        return carry

    lax.fori_loop(0, n_mine, finish, 0)


SMEM = pl.BlockSpec(memory_space=pltpu.SMEM)
VMEM = pl.BlockSpec(memory_space=pltpu.VMEM)
HBM = pl.BlockSpec(memory_space=pltpu.HBM)
ANY = pl.BlockSpec(memory_space=pl.ANY)


def pick(room, pivots, trailing):
    return pl.pallas_call(
        functools.partial(pick_kernel, room),
        out_shape=jax.ShapeDtypeStruct((N_PROW, NB + room, LANES), F32),
        in_specs=[SMEM, HBM],
        out_specs=VMEM,
        scratch_shapes=[
            pltpu.SMEM((ROWS,), jnp.int32),
            pltpu.SMEM((1,), jnp.int32),
            pltpu.SMEM((2 * NB + 2,), jnp.int32),
            pltpu.SemaphoreType.DMA,
            pltpu.SemaphoreType.DMA((N_PROW,)),
        ],
        compiler_params=pltpu.CompilerParams(vmem_limit_bytes=58 * 2**20),
    )(pivots, trailing)


def join_kernel(mine, other, pair):
    pair[0:NB, :] = mine[...]
    pair[NB : 2 * NB, :] = other[...]


def join(mine, other):
    return pl.pallas_call(
        join_kernel,
        out_shape=jax.ShapeDtypeStruct((2 * NB, LANES), F32),
        in_specs=[VMEM, VMEM],
        out_specs=VMEM,
        compiler_params=pltpu.CompilerParams(vmem_limit_bytes=8 * 2**20),
    )(mine, other)


MOVED = NB
ROUTES = 3 * NB
OWN = 2 * NB


def route_kernel(room, pivots, routes, owned, over, table, own, order, count, sems):
    send_rows, back_rows = NB + room, NB + room + LOWER
    me = lax.axis_index("prow")
    for q in range(N_PROW + 1):
        count[q] = 0

    def visit(j, row):
        holder = holder_of(row)
        extra = count[N_PROW]
        count[N_PROW] = extra + jnp.where(jnp.logical_and(holder == 0, row >= NB), 1, 0)
        spare = NB + jnp.minimum(extra, room - 1)
        slot = jnp.where(holder == 0, jnp.where(row < NB, row, spare), j)
        table[0, j] = holder * send_rows + slot

    swap_chain(pivots, order, visit)

    for j in range(NB):
        row = pivots[j]
        outside = row >= NB
        q = jnp.where(outside, holder_of(row), 0)
        slot = count[q]
        count[q] = slot + jnp.where(outside, 1, 0)
        fits = jnp.logical_and(outside, slot < room)
        table[0, MOVED + 2 * j] = jnp.where(fits, q * back_rows + NB + slot, 0)
        table[0, MOVED + 2 * j + 1] = jnp.where(outside, order[row], 0)
        here = jnp.logical_and(outside, q == me)
        own[0, jnp.where(here, 1 + slot, OWN - 1)] = local_of(row)

    own[0, 0] = jnp.minimum(count[me], room)
    most = count[N_PROW]
    for q in range(N_PROW):
        most = jnp.maximum(most, count[q])
    over[0] = jnp.where(most > room, 1, 0)
    first = pltpu.make_async_copy(table, routes, sems.at[0])
    second = pltpu.make_async_copy(own, owned, sems.at[1])
    first.start()
    second.start()
    first.wait()
    second.wait()


def route(room, pivots):
    return pl.pallas_call(
        functools.partial(route_kernel, room),
        out_shape=(
            jax.ShapeDtypeStruct((1, ROUTES), jnp.int32),
            jax.ShapeDtypeStruct((1, OWN), jnp.int32),
            jax.ShapeDtypeStruct((1,), jnp.int32),
        ),
        in_specs=[SMEM],
        out_specs=(VMEM, VMEM, SMEM),
        scratch_shapes=[
            pltpu.SMEM((1, ROUTES), jnp.int32),
            pltpu.SMEM((1, OWN), jnp.int32),
            pltpu.SMEM((ROWS,), jnp.int32),
            pltpu.SMEM((N_PROW + 1,), jnp.int32),
            pltpu.SemaphoreType.DMA((2,)),
        ],
        compiler_params=pltpu.CompilerParams(vmem_limit_bytes=8 * 2**20),
    )(pivots)


HALF = NB // 2


def fold(diagonal):
    row_id = lax.broadcasted_iota(jnp.int32, (HALF, HALF), 0)
    col_id = lax.broadcasted_iota(jnp.int32, (HALF, HALF), 1)
    first = diagonal[0:HALF, 0:HALF]
    last = diagonal[HALF:NB, HALF:NB]
    mixed = jnp.where(col_id > row_id, first, last.T)
    both = jnp.concatenate([mixed, diagonal[0:HALF, HALF:NB]], axis=1)
    return jnp.concatenate([both[0:LOWER], both[LOWER:HALF]], axis=1)


def unfold(packed):
    row_id = lax.broadcasted_iota(jnp.int32, (HALF, HALF), 0)
    col_id = lax.broadcasted_iota(jnp.int32, (HALF, HALF), 1)
    both = jnp.concatenate([packed[:, 0:NB], packed[:, NB:LANES]], axis=0)
    mixed = both[:, 0:HALF]
    zero = jnp.zeros((HALF, HALF), F32)
    first = jnp.where(col_id < row_id, mixed.T, zero)
    last = jnp.where(col_id < row_id, mixed, zero)
    top = jnp.concatenate([first, zero], axis=1)
    return jnp.concatenate([top, jnp.concatenate([both[:, HALF:NB].T, last], axis=1)], axis=0)


def spread_kernel(
    room, routes, got, mine, other, below, above, across, back, table, diagonal, sem
):
    copy = pltpu.make_async_copy(routes, table, sem)
    copy.start()
    back_rows = NB + room + LOWER
    c = lax.axis_index("pcol")
    z, core = c // 2, c % 2
    start = pl.multiple_of(core * NB, NB)

    @pl.when(c == 0)
    def _():
        diagonal[...] = mine[...]

    @pl.when(c == 1)
    def _():
        diagonal[...] = other[...]

    for place, pair in ((1, below), (2, across), (3, above)):

        @pl.when(z == place)
        def _():
            diagonal[...] = pair[pl.ds(start, NB), :]

    packed = fold(diagonal[:, 0:NB])
    for q in range(N_PROW):
        low = q * back_rows + NB + room
        back[low : low + LOWER, :] = packed
    copy.wait()

    for j in range(NB):
        source = got[pl.ds(table[0, MOVED + 2 * j + 1], 1), :]
        back[pl.ds(table[0, MOVED + 2 * j], 1), :] = source
    for j in range(NB):
        back[j : j + 1, :] = got[pl.ds(table[0, j], 1), :]
    for q in range(1, N_PROW):
        base = q * back_rows
        back[base : base + NB, :] = back[0:NB, :]


def spread(room, routes, got, panels):
    back_rows = NB + room + LOWER
    return pl.pallas_call(
        functools.partial(spread_kernel, room),
        out_shape=jax.ShapeDtypeStruct((N_PROW * back_rows, LANES), F32),
        in_specs=[ANY] + [VMEM] * 6,
        out_specs=VMEM,
        scratch_shapes=[
            pltpu.SMEM((1, ROUTES), jnp.int32),
            pltpu.VMEM((NB, LANES), F32),
            pltpu.SemaphoreType.DMA,
        ],
        compiler_params=pltpu.CompilerParams(vmem_limit_bytes=16 * 2**20),
    )(routes, got, *panels)


def halves(x):
    high = x.astype(BF16)
    return high, (x - high.astype(F32)).astype(BF16)


def thirds(x):
    high = x.astype(BF16)
    rest = x - high.astype(F32)
    mid = rest.astype(BF16)
    return high, mid, (rest - mid.astype(F32)).astype(BF16)


HEAD = 256
WIDEST = 512
CHUNKS = ((0, HEAD), (256, 512), (768, 512), (1280, 512), (1792, 256))


def prepare_kernel(back, trailing, mine, other, below, above, across, head, multipliers, sem):
    del back
    c = lax.axis_index("pcol")
    z, core = c // 2, c % 2
    load = pltpu.make_async_copy(trailing.at[:, pl.ds(0, HEAD)], head, sem)
    load.start()

    def place(step, side, values):
        high, low = halves(values.T)
        start = (((z + step) & 3) * 2 + ((core + side) & 1)) * LANES
        rows = pl.ds(pl.multiple_of(start, LANES), LANES)
        multipliers[rows, :] = jnp.concatenate([high, low, high, low], axis=1)

    place(0, 0, mine[...])
    place(0, 1, other[...])
    for step, pair in ((3, below), (1, above), (2, across)):
        place(step, 0, pair[0:NB, :])
        place(step, 1, pair[NB : 2 * NB, :])
    load.wait()


def prepare(back, trailing, panels):
    rows, cols = trailing.shape
    return pl.pallas_call(
        prepare_kernel,
        out_shape=(
            jax.ShapeDtypeStruct((rows, HEAD), F32),
            jax.ShapeDtypeStruct((rows, 4 * NB), BF16),
        ),
        in_specs=[ANY, HBM] + [VMEM] * 5,
        out_specs=(VMEM, VMEM),
        scratch_shapes=[pltpu.SemaphoreType.DMA],
        compiler_params=pltpu.CompilerParams(vmem_limit_bytes=24 * 2**20),
        cost_estimate=pl.CostEstimate(flops=0, bytes_accessed=4 * rows * cols, transcendentals=0),
    )(back, trailing, *panels)


def update_kernel(
    room, owned, given, multipliers, head, trailing, updated, block, products, own, columns, arrive, leave, sem
):
    back_rows = NB + room + LOWER
    me = lax.axis_index("prow")

    def load(k):
        cols = pl.ds(*CHUNKS[k])
        return pltpu.make_async_copy(trailing.at[:, cols], block.at[:, cols], arrive.at[k])

    def store(k):
        cols = pl.ds(*CHUNKS[k])
        return pltpu.make_async_copy(block.at[:, cols], updated.at[:, cols], leave.at[k])

    copy = pltpu.make_async_copy(owned, own, sem)
    copy.start()
    for k in range(1, len(CHUNKS)):
        load(k).start()

    lower = unfold(given[NB + room : back_rows, :])
    for j in range(NB):
        columns[j] = jnp.broadcast_to(lower[:, j : j + 1], (NB, LANES))

    row_id = lax.broadcasted_iota(jnp.int32, (8, LANES), 0)
    col_id = lax.broadcasted_iota(jnp.int32, (8, LANES), 1)
    inverse = [jnp.where(col_id == row_id + 8 * b, 1.0, 0.0).astype(F32) for b in range(8)]
    for j in range(NB):
        b, s = j // 8, j % 8
        row = jnp.broadcast_to(inverse[b][s : s + 1, :], (8, LANES))
        for i in range(b, 8):
            inverse[i] = inverse[i] - columns[j, 8 * i : 8 * i + 8, :] * row
    inv_high, inv_mid, inv_low = thirds(jnp.concatenate(inverse, axis=0)[:, 0:NB])
    left = jnp.concatenate([inv_high, inv_mid, inv_low, inv_high, inv_mid, inv_high], axis=1)

    copy.wait()
    n_own = own[0, 0]
    for k, (start, width) in enumerate(CHUNKS):
        cols = slice(start, start + width)
        pieces = range(start // LANES, (start + width) // LANES)
        swapped = jnp.concatenate(
            [given[p * back_rows : p * back_rows + NB, :] for p in pieces], axis=1
        )
        high, mid, low = thirds(swapped)
        right = jnp.concatenate([high, high, high, mid, mid, low], axis=0)
        upper = jnp.dot(left, right, preferred_element_type=F32)
        up_high, up_low = halves(upper)
        factor = jnp.concatenate([up_high, up_high, up_low, up_low], axis=0)

        part = slice(0, width)
        products[:, part] = jnp.dot(multipliers[...], factor, preferred_element_type=F32)
        if k == 0:
            block[:, cols] = head[...] - products[:, part]
        else:
            load(k).wait()
            block[:, cols] = block[:, cols] - products[:, part]

        def displace(slot, carry):
            row = own[0, 1 + slot]
            group = pl.ds(pl.multiple_of(row // 8 * 8, 8), 8)
            for n, p in enumerate(pieces):
                moved = given[pl.ds(p * back_rows + NB + slot, 1), :]
                part = slice(p * LANES, (p + 1) * LANES)
                change = moved - products[group, n * LANES : (n + 1) * LANES]
                block[group, part] = jnp.where(row_id == row % 8, change, block[group, part])
            return carry

        lax.fori_loop(0, n_own, displace, 0)

        @pl.when(me == 0)
        def _():
            block[0:NB, cols] = upper

        store(k).start()
    for k in range(len(CHUNKS)):
        store(k).wait()


def update(room, owned, given, multipliers, head, trailing):
    rows, cols = trailing.shape
    return pl.pallas_call(
        functools.partial(update_kernel, room),
        out_shape=jax.ShapeDtypeStruct((rows, cols), F32),
        in_specs=[VMEM] * 4 + [HBM],
        out_specs=HBM,
        scratch_shapes=[
            pltpu.VMEM((rows, cols), F32),
            pltpu.VMEM((rows, WIDEST), F32),
            pltpu.SMEM((1, OWN), jnp.int32),
            pltpu.VMEM((NB, NB, LANES), F32),
            pltpu.SemaphoreType.DMA((len(CHUNKS),)),
            pltpu.SemaphoreType.DMA((len(CHUNKS),)),
            pltpu.SemaphoreType.DMA,
        ],
        compiler_params=pltpu.CompilerParams(vmem_limit_bytes=48 * 2**20),
    )(owned, given, multipliers, head, trailing)


def ring(step):
    return [(c, (c // 2 + step) % 4 * 2 + c % 2) for c in range(N_PCOL)]


def step(room, trailing, factors, partner, pivots):
    sent = pick(room, pivots, trailing)
    got = lax.all_to_all(sent, "prow", 0, 0)
    pair = join(factors, partner)
    below = lax.ppermute(pair, "pcol", ring(1))
    above = lax.ppermute(pair, "pcol", ring(3))
    across = lax.ppermute(pair, "pcol", ring(2))
    routes, owned, over = route(room, pivots)
    panels = (factors, partner, below, above, across)
    back = spread(room, routes, got.reshape(-1, LANES), panels)
    given = lax.all_to_all(back.reshape(N_PROW, -1, LANES), "prow", 0, 0)
    head, multipliers = prepare(back, trailing, panels)
    updated = update(room, owned, given.reshape(-1, LANES), multipliers, head, trailing)
    return updated, over


def body(trailing, factors, pivots):
    partner = lax.ppermute(factors, "pcol", [(c, c ^ 1) for c in range(N_PCOL)])
    updated, over = step(FEW, trailing, factors, partner, pivots)

    def again(updated):
        return step(NB, trailing, factors, partner, pivots)[0]

    return lax.cond(over[0] == 0, lambda updated: updated, again, updated)


def solution(mesh):
    return jax.shard_map(
        body,
        mesh=mesh,
        in_specs=(P("prow", "pcol"), P(None, ("prow", "pcol")), P()),
        out_specs=P("prow", "pcol"),
        check_vma=False,
    )
```

time: 56.5 us -> 50.5 us (0.89)
  blocking collectives: 18.5 us -> 0 us
  waiting for transfers between devices: 5.41 us -> 14.9 us
  starting transfers between devices: 13.3 us -> 18.6 us
  local copies, waits for them, and re-layouts: 2.09 us -> 0.01 us
    all_to_all x1 -> x0, blocking collectives: 18.5 us -> none  [rest(): given = lax.all_to_all(back.reshape(N_PROW, -1, LANES), 'prow', 0, 0)]
    all_to_all x1 -> x2, waiting for transfers between devices: 1.04 us -> 12.3 us  [the longest x1 10.8 us: step(): given = lax.all_to_all(back.reshape(N_PROW, -1, LANES), 'prow', 0, 0)]
    all_to_all x1 -> x2, starting transfers between devices: 7.28 us -> 12.6 us  [the longest x1 6.91 us: step(): got = lax.all_to_all(sent, 'prow', 0, 0)]
    ppermute x3, waiting for transfers between devices: 4.37 us -> 1.34 us  [the longest x1 1.34 us: step(): below = lax.ppermute(pair, 'pcol', ring(1))]
    pallas_call x1, Pallas kernels: 8.61 us -> 6.04 us  [update(): pl.pallas_call(functools.partial(update_kernel, room), out_shape=jax.Shap...]
    cond x10 -> x0, local copies, waits for them, and re-layouts: 1.51 us -> none
    pallas_call x1 -> x3, Pallas kernels: 3.65 us -> 5.03 us  [the longest x1 3.54 us: pick(): pl.pallas_call(functools.partial(pick_kernel, room), out_shape=jax.ShapeD...]
    ppermute x1, waiting for transfers between devices: 0.01 us -> 1.19 us  [body(): partner = lax.ppermute(factors, 'pcol', [(c, c ^ 1) for c in range(N_PCOL)])]
  transfers between devices with their start and end apart: 5 -> 6, of which waited for: 4 -> 4; matrix products, arithmetic and copies ran while one was open for 1% -> 0% of each run, Pallas kernels for 10% -> 9%
where the time goes in v3:
time: 50.5 us; the launch traced here: 50.1 us
  starting transfers between devices  18.6 us (37%)
  Pallas kernels  15.4 us (30%)
  waiting for transfers between devices  14.9 us (30%)
  between operations  0.9 us (2%)
    all_to_all x1, waiting for transfers between devices, step(): given = lax.all_to_all(back.reshape(N_PROW, -1, LANES), 'prow', 0, 0)  10.8 us
    all_to_all x1, starting transfers between devices, step(): got = lax.all_to_all(sent, 'prow', 0, 0)  6.91 us
    pallas_call x1, Pallas kernels, update(): pl.pallas_call(functools.partial(update_kernel, room), out_shape=jax.Shap...  6.04 us
    all_to_all x1, starting transfers between devices, step(): given = lax.all_to_all(back.reshape(N_PROW, -1, LANES), 'prow', 0, 0)  5.71 us
    ppermute x1, starting transfers between devices, step(): across = lax.ppermute(pair, 'pcol', ring(2))  3.88 us
    pallas_call x1, Pallas kernels, pick(): pl.pallas_call(functools.partial(pick_kernel, room), out_shape=jax.ShapeD...  3.54 us
    pallas_call x1, Pallas kernels, route(): pl.pallas_call(functools.partial(route_kernel, room), out_shape=(jax.Shap...  2.79 us
    pallas_call x1, Pallas kernels, spread(): pl.pallas_call(functools.partial(spread_kernel, room), out_shape=jax.Shap...  1.58 us
  transfers between devices with their start and end apart: 6, of which 4 were waited for; matrix products, arithmetic and copies ran while one was open for 0% of the time, Pallas kernels for 9%

profile of v3, /device:TPU:0, one launch (start us, length us, event | category | flops | bytes accessed | tf_op | source)
XLA Modules:
  0.0 50.1 jit_solution(15663498157538846554)
XLA Ops:
  0.0 0.0 copy-start.1
  0.0 0.0 copy-start
  0.0 3.5 %shard_map.40 = f32[16,80,128]{2,1,0:T(8,128)} custom-call(s32[64]{0:T(128)} %pivots.3, f32[1024,2048]{1,0:T(8,128)} %trailing.5), custom_call_target="tpu_custom_call" | custom-call | tf_op jit(solution)/shard_map/pallas_call | solution.py:102
  3.6 6.9 %all-to-all-start.2 = ((f32[16,80,128]{2,1,0:T(8,128)}), f32[16,80,128]{2,1,0:T(8,128)S(1)}, u32[]{:S(2)}, u32[]{:S(2)}) async-start(f32[16,80,128]{2,1,0:T(8,128)} %shard_map.40), calls=%async_computation.2 | async-start | bytes 1310720 | tf_op jit(solution)/shard_map/all_to_all | solution.py:438
  10.5 0.0 copy-done
  10.5 0.1 collective-permute-start.3
  10.6 1.2 %collective-permute-done.3.other = f32[64,128]{1,0:T(8,128)S(1)} collective-permute-done((f32[64,128]{1,0:T(8,128)S(1)}, f32[64,128]{1,0:T(8,128)S(1)}, u32[]{:S(2)}, u32[]{:S(2)}) %collective-permute-start.3) | collective-permute-done | bytes 32800 | tf_op jit(solution)/shard_map/ppermute | solution.py:453
  11.8 3.9 %collective-permute-start.6 = (f32[128,128]{1,0:T(8,128)S(1)}, f32[128,128]{1,0:T(8,128)S(1)}, u32[]{:S(2)}, u32[]{:S(2)}) collective-permute-start(f32[128,128]{1,0:T(8,128)S(1)} %shard_map.41), channel_id=1, source_target_pairs={{0,4},{1,5},{2,6},{3,7},{4,0},{5,1},{6,2},{7,3},{8,12},{9,13},{10,... | collective-permute-start | bytes 196616 | tf_op jit(solution)/shard_map/ppermute | solution.py:442
  15.7 0.7 %collective-permute-start.5 = (f32[128,128]{1,0:T(8,128)S(1)}, f32[128,128]{1,0:T(8,128)S(1)}, u32[]{:S(2)}, u32[]{:S(2)}) collective-permute-start(f32[128,128]{1,0:T(8,128)S(1)} %shard_map.41), channel_id=1, source_target_pairs={{0,6},{1,7},{2,0},{3,1},{4,2},{5,3},{6,4},{7,5},{8,14},{9,15},{10,... | collective-permute-start | bytes 196616 | tf_op jit(solution)/shard_map/ppermute | solution.py:441
  16.4 1.3 %collective-permute-start.4 = (f32[128,128]{1,0:T(8,128)S(1)}, f32[128,128]{1,0:T(8,128)S(1)}, u32[]{:S(2)}, u32[]{:S(2)}) collective-permute-start(f32[128,128]{1,0:T(8,128)S(1)} %shard_map.41), channel_id=1, source_target_pairs={{0,2},{1,3},{2,4},{3,5},{4,6},{5,7},{6,0},{7,1},{8,10},{9,11},{10,... | collective-permute-start | bytes 196616 | tf_op jit(solution)/shard_map/ppermute | solution.py:440
  17.7 0.0 copy-done.1
  17.7 2.8 %shard_map.39 = (s32[1,192]{1,0:T(1,128)S(1)}, s32[1,128]{1,0:T(1,128)S(1)}, s32[1]{0:T(128)}) custom-call(s32[64]{0:T(128)S(1)} %copy-done.1), custom_call_target="tpu_custom_call" | custom-call | tf_op jit(solution)/shard_map/pallas_call | solution.py:180
  20.5 0.0 collective-permute-done.6.across
  20.5 0.0 collective-permute-done.5.above
  20.5 1.3 %collective-permute-done.4.below = f32[128,128]{1,0:T(8,128)S(1)} collective-permute-done((f32[128,128]{1,0:T(8,128)S(1)}, f32[128,128]{1,0:T(8,128)S(1)}, u32[]{:S(2)}, u32[]{:S(2)}) %collective-permute-start.4) | collective-permute-done | bytes 65568 | tf_op jit(solution)/shard_map/ppermute | solution.py:440
  21.8 1.5 %all-to-all-done.2 = f32[16,80,128]{2,1,0:T(8,128)S(1)} async-done(((f32[16,80,128]{2,1,0:T(8,128)}), f32[16,80,128]{2,1,0:T(8,128)S(1)}, u32[]{:S(2)}, u32[]{:S(2)}) %all-to-all-start.2) | async-done | bytes 655392 | tf_op jit(solution)/shard_map/all_to_all | solution.py:438
  23.4 1.6 %shard_map.42.back = f32[1536,128]{1,0:T(8,128)} custom-call(s32[1,192]{1,0:T(1,128)S(1)} %get-tuple-element.32.routes, f32[1280,128]{1,0:T(8,128)S(1)} %bitcast.10, f32[64,128]{1,0:T(8,128)S(1)} %copy-done, f32[64,128]{1,0:T(8,128)S(1)} %collective-permute-done.3.other, f32[128,128]{1,0:T(8,128)S(1)} %collective-permute-done.4.below, ...), custom_call_target="tpu_custom_call" | custom-call | tf_op jit(solution)/shard_map/pallas_call | solution.py:267
  25.0 5.7 %all-to-all-start.3 = ((f32[16,96,128]{2,1,0:T(8,128)}), f32[16,96,128]{2,1,0:T(8,128)S(1)}, u32[]{:S(2)}, u32[]{:S(2)}) async-start(f32[16,96,128]{2,1,0:T(8,128)} %bitcast.5), calls=%async_computation.3 | async-start | bytes 1572864 | tf_op jit(solution)/shard_map/all_to_all | solution.py:446
  31.3 1.5 %shard_map.43 = (f32[1024,256]{1,0:T(8,128)S(1)}, bf16[1024,256]{1,0:T(8,128)(2,1)S(1)}) custom-call(f32[1536,128]{1,0:T(8,128)} %shard_map.42.back, f32[1024,2048]{1,0:T(8,128)} %trailing.5, f32[64,128]{1,0:T(8,128)S(1)} %copy-done, f32[64,128]{1,0:T(8,128)S(1)} %collective-permute-done.3.other, f32[128,128]{1,0:T(8,128)S(1)} %collective-permute-done.4.below, ...), custom_call_target="tpu_custom_call" | custom-call | bytes 8388608 | tf_op jit(solution)/shard_map/pallas_call | solution.py:321
  32.8 10.8 %all-to-all-done.3 = f32[16,96,128]{2,1,0:T(8,128)S(1)} async-done(((f32[16,96,128]{2,1,0:T(8,128)}), f32[16,96,128]{2,1,0:T(8,128)S(1)}, u32[]{:S(2)}, u32[]{:S(2)}) %all-to-all-start.3) | async-done | bytes 786464 | tf_op jit(solution)/shard_map/all_to_all | solution.py:446
  43.6 6.0 %shard_map.44 = f32[1024,2048]{1,0:T(8,128)} custom-call(s32[1,128]{1,0:T(1,128)S(1)} %get-tuple-element.31.owned, f32[1536,128]{1,0:T(8,128)S(1)} %bitcast.9, bf16[1024,256]{1,0:T(8,128)(2,1)S(1)} %get-tuple-element.33.multipliers, f32[1024,256]{1,0:T(8,128)S(1)} %get-tuple-element.34.head, f32[1024,2048]{1,0:T(8,128)} %trailing.5), custom_call_target="tpu_custom_call" | custom-call | tf_op jit(solution)/shard_map/pallas_call | solution.py:414
  49.6 0.2 conditional.1
  (1 shorter events, 0.0 us)
Async XLA Ops:
  0.0 17.7 %copy-start.1 = (s32[64]{0:T(128)S(1)}, s32[64]{0:T(128)}, u32[]{:S(2)}) copy-start(s32[64]{0:T(128)} %pivots.3) | copy-start | bytes 772
  0.0 10.5 %copy-start = (f32[64,128]{1,0:T(8,128)S(1)}, f32[64,128]{1,0:T(8,128)}, u32[]{:S(2)}) copy-start(f32[64,128]{1,0:T(8,128)} %mine.5) | copy-start | bytes 98308
  3.6 19.8 %all-to-all-start.2 = ((f32[16,80,128]{2,1,0:T(8,128)}), f32[16,80,128]{2,1,0:T(8,128)S(1)}, u32[]{:S(2)}, u32[]{:S(2)}) async-start(f32[16,80,128]{2,1,0:T(8,128)} %shard_map.40), calls=%async_computation.2 | async-start | bytes 1310720 | tf_op jit(solution)/shard_map/all_to_all | solution.py:438
  10.5 1.3 %collective-permute-start.3 = (f32[64,128]{1,0:T(8,128)S(1)}, f32[64,128]{1,0:T(8,128)S(1)}, u32[]{:S(2)}, u32[]{:S(2)}) collective-permute-start(f32[64,128]{1,0:T(8,128)S(1)} %copy-done), channel_id=1, source_target_pairs={{0,1},{1,0},{2,3},{3,2},{4,5},{5,4},{6,7},{7,6},{8,9},{9,8},{10,11... | collective-permute-start | bytes 98312 | tf_op jit(solution)/shard_map/ppermute | solution.py:453
  11.8 8.7 %collective-permute-start.6 = (f32[128,128]{1,0:T(8,128)S(1)}, f32[128,128]{1,0:T(8,128)S(1)}, u32[]{:S(2)}, u32[]{:S(2)}) collective-permute-start(f32[128,128]{1,0:T(8,128)S(1)} %shard_map.41), channel_id=1, source_target_pairs={{0,4},{1,5},{2,6},{3,7},{4,0},{5,1},{6,2},{7,3},{8,12},{9,13},{10,... | collective-permute-start | bytes 196616 | tf_op jit(solution)/shard_map/ppermute | solution.py:442
  15.7 4.8 %collective-permute-start.5 = (f32[128,128]{1,0:T(8,128)S(1)}, f32[128,128]{1,0:T(8,128)S(1)}, u32[]{:S(2)}, u32[]{:S(2)}) collective-permute-start(f32[128,128]{1,0:T(8,128)S(1)} %shard_map.41), channel_id=1, source_target_pairs={{0,6},{1,7},{2,0},{3,1},{4,2},{5,3},{6,4},{7,5},{8,14},{9,15},{10,... | collective-permute-start | bytes 196616 | tf_op jit(solution)/shard_map/ppermute | solution.py:441
  16.4 5.5 %collective-permute-start.4 = (f32[128,128]{1,0:T(8,128)S(1)}, f32[128,128]{1,0:T(8,128)S(1)}, u32[]{:S(2)}, u32[]{:S(2)}) collective-permute-start(f32[128,128]{1,0:T(8,128)S(1)} %shard_map.41), channel_id=1, source_target_pairs={{0,2},{1,3},{2,4},{3,5},{4,6},{5,7},{6,0},{7,1},{8,10},{9,11},{10,... | collective-permute-start | bytes 196616 | tf_op jit(solution)/shard_map/ppermute | solution.py:440
  25.0 18.6 %all-to-all-start.3 = ((f32[16,96,128]{2,1,0:T(8,128)}), f32[16,96,128]{2,1,0:T(8,128)S(1)}, u32[]{:S(2)}, u32[]{:S(2)}) async-start(f32[16,96,128]{2,1,0:T(8,128)} %bitcast.5), calls=%async_computation.3 | async-start | bytes 1572864 | tf_op jit(solution)/shard_map/all_to_all | solution.py:446

commit v4 on v3

v4 whole, which is shorter than its diff:
```python
import jax
import jax.numpy as jnp
from jax import lax
from jax.experimental import pallas as pl
from jax.experimental.pallas import tpu as pltpu
from jax.sharding import PartitionSpec as P

LANES = 128
NB = 64
N_PROW = 16
N_PCOL = 8
ROWS = 16384
LOWER = 16
BACK = NB + LOWER
F32 = jnp.float32
BF16 = jnp.bfloat16


def holder_of(row):
    return (row >> 6) & (N_PROW - 1)


def local_of(row):
    return ((row >> 10) << 6) | (row & (NB - 1))


def swap_chain(pivots, order, visit):
    for j in range(NB):
        order[pivots[j]] = pivots[j]
    for j in range(NB):
        order[j] = j
    for j in range(NB):
        k = pivots[j]
        row = order[k]
        order[k] = order[j]
        visit(j, row)


def pick_kernel(pivots, trailing, sent, order, count, rows, slots, sem, top_sem):
    me = lax.axis_index("prow")

    def row_copy(row, slot, piece):
        return pltpu.make_async_copy(
            trailing.at[pl.ds(row, 1), pl.ds(piece * LANES, LANES)],
            sent.at[piece, pl.ds(slot, 1), :],
            sem,
        )

    def top_copy(piece):
        return pltpu.make_async_copy(
            trailing.at[pl.ds(0, NB), pl.ds(piece * LANES, LANES)],
            sent.at[piece, pl.ds(0, NB), :],
            top_sem.at[piece],
        )

    @pl.when(me == 0)
    def _():
        for piece in range(N_PROW):
            top_copy(piece).start()

    count[0] = 0

    def visit(j, row):
        place = count[0]
        rows[place] = row
        slots[place] = j
        wanted = jnp.logical_and(holder_of(row) == me, row >= NB)
        count[0] = place + jnp.where(wanted, 1, 0)

    swap_chain(pivots, order, visit)
    n_mine = count[0]

    @pl.when(me == 0)
    def _():
        for piece in range(N_PROW):
            top_copy(piece).wait()

    def send(i, carry):
        row = rows[i]
        slot = jnp.where(me == 0, order[row], slots[i])
        for piece in range(N_PROW):
            row_copy(local_of(row), slot, piece).start()
        return carry

    lax.fori_loop(0, n_mine, send, 0)

    def finish(i, carry):
        for piece in range(N_PROW):
            row_copy(0, 0, piece).wait()
        return carry

    lax.fori_loop(0, n_mine, finish, 0)


SMEM = pl.BlockSpec(memory_space=pltpu.SMEM)
VMEM = pl.BlockSpec(memory_space=pltpu.VMEM)
HBM = pl.BlockSpec(memory_space=pltpu.HBM)
ANY = pl.BlockSpec(memory_space=pl.ANY)


def pick(pivots, trailing):
    return pl.pallas_call(
        pick_kernel,
        out_shape=jax.ShapeDtypeStruct((N_PROW, NB, LANES), F32),
        in_specs=[SMEM, HBM],
        out_specs=VMEM,
        scratch_shapes=[
            pltpu.SMEM((ROWS,), jnp.int32),
            pltpu.SMEM((1,), jnp.int32),
            pltpu.SMEM((NB + 1,), jnp.int32),
            pltpu.SMEM((NB + 1,), jnp.int32),
            pltpu.SemaphoreType.DMA,
            pltpu.SemaphoreType.DMA((N_PROW,)),
        ],
        compiler_params=pltpu.CompilerParams(vmem_limit_bytes=58 * 2**20),
    )(pivots, trailing)


def join_kernel(mine, other, pair):
    pair[0:NB, :] = mine[...]
    pair[NB : 2 * NB, :] = other[...]


def join(mine, other):
    return pl.pallas_call(
        join_kernel,
        out_shape=jax.ShapeDtypeStruct((2 * NB, LANES), F32),
        in_specs=[VMEM, VMEM],
        out_specs=VMEM,
        compiler_params=pltpu.CompilerParams(vmem_limit_bytes=8 * 2**20),
    )(mine, other)


TARGET = NB
SOURCE = 2 * NB
ROUTES = 3 * NB
OWN = 2 * NB


def route_kernel(pivots, routes, owned, table, own, order, rows, count, sems):
    me = lax.axis_index("prow")

    def visit(j, row):
        rows[j] = row

    swap_chain(pivots, order, visit)
    count[0] = 0
    for j in range(NB):
        row = rows[j]
        holder = holder_of(row)
        outside = row >= NB
        displacer = jnp.where(outside, order[row], row)
        place = holder * NB + jnp.where(holder == 0, displacer, j)
        away = holder > 0
        table[0, j] = place
        table[0, TARGET + j] = holder * BACK + j
        table[0, SOURCE + j] = jnp.where(away, displacer, place)
        slot = count[0]
        own[0, 1 + slot] = local_of(row) * NB + jnp.where(away, j, displacer)
        count[0] = slot + jnp.where(jnp.logical_and(outside, holder == me), 1, 0)
    own[0, 0] = count[0]
    first = pltpu.make_async_copy(table, routes, sems.at[0])
    second = pltpu.make_async_copy(own, owned, sems.at[1])
    first.start()
    second.start()
    first.wait()
    second.wait()


def route(pivots):
    return pl.pallas_call(
        route_kernel,
        out_shape=(
            jax.ShapeDtypeStruct((1, ROUTES), jnp.int32),
            jax.ShapeDtypeStruct((1, OWN), jnp.int32),
        ),
        in_specs=[SMEM],
        out_specs=(VMEM, VMEM),
        scratch_shapes=[
            pltpu.SMEM((1, ROUTES), jnp.int32),
            pltpu.SMEM((1, OWN), jnp.int32),
            pltpu.SMEM((ROWS,), jnp.int32),
            pltpu.SMEM((NB,), jnp.int32),
            pltpu.SMEM((1,), jnp.int32),
            pltpu.SemaphoreType.DMA((2,)),
        ],
        compiler_params=pltpu.CompilerParams(vmem_limit_bytes=8 * 2**20),
    )(pivots)


HALF = NB // 2


def fold(diagonal):
    row_id = lax.broadcasted_iota(jnp.int32, (HALF, HALF), 0)
    col_id = lax.broadcasted_iota(jnp.int32, (HALF, HALF), 1)
    first = diagonal[0:HALF, 0:HALF]
    last = diagonal[HALF:NB, HALF:NB]
    mixed = jnp.where(col_id > row_id, first, last.T)
    both = jnp.concatenate([mixed, diagonal[0:HALF, HALF:NB]], axis=1)
    return jnp.concatenate([both[0:LOWER], both[LOWER:HALF]], axis=1)


def unfold(packed):
    row_id = lax.broadcasted_iota(jnp.int32, (HALF, HALF), 0)
    col_id = lax.broadcasted_iota(jnp.int32, (HALF, HALF), 1)
    both = jnp.concatenate([packed[:, 0:NB], packed[:, NB:LANES]], axis=0)
    mixed = both[:, 0:HALF]
    zero = jnp.zeros((HALF, HALF), F32)
    first = jnp.where(col_id < row_id, mixed.T, zero)
    last = jnp.where(col_id < row_id, mixed, zero)
    top = jnp.concatenate([first, zero], axis=1)
    return jnp.concatenate([top, jnp.concatenate([both[:, HALF:NB].T, last], axis=1)], axis=0)


def spread_kernel(routes, got, *refs):
    panels, (back, table, diagonal, sem) = refs[:5], refs[5:]
    copy = pltpu.make_async_copy(routes, table, sem)
    copy.start()
    c = lax.axis_index("pcol")
    start = pl.multiple_of(c % 2 * NB, NB)
    for side in range(2):

        @pl.when(c == side)
        def _():
            diagonal[...] = panels[side][...]

    for step, pair in enumerate(panels[2:], 1):

        @pl.when(c // 2 == 4 - step)
        def _():
            diagonal[...] = pair[pl.ds(start, NB), :]

    packed = fold(diagonal[:, 0:NB])
    for q in range(N_PROW):
        low = q * BACK + NB
        back[low : low + LOWER, :] = packed
    copy.wait()
    for j in range(NB):
        back[j : j + 1, :] = got[pl.ds(table[0, j], 1), :]
    for q in range(1, N_PROW):
        back[q * BACK : q * BACK + NB, :] = back[0:NB, :]
    for j in range(NB):
        source = got[pl.ds(table[0, SOURCE + j], 1), :]
        back[pl.ds(table[0, TARGET + j], 1), :] = source


def spread(routes, got, panels):
    return pl.pallas_call(
        spread_kernel,
        out_shape=jax.ShapeDtypeStruct((N_PROW * BACK, LANES), F32),
        in_specs=[ANY] + [VMEM] * 6,
        out_specs=VMEM,
        scratch_shapes=[
            pltpu.SMEM((1, ROUTES), jnp.int32),
            pltpu.VMEM((NB, LANES), F32),
            pltpu.SemaphoreType.DMA,
        ],
        compiler_params=pltpu.CompilerParams(vmem_limit_bytes=16 * 2**20),
    )(routes, got, *panels)


def halves(x):
    high = x.astype(BF16)
    return high, (x - high.astype(F32)).astype(BF16)


def thirds(x):
    high = x.astype(BF16)
    rest = x - high.astype(F32)
    mid = rest.astype(BF16)
    return high, mid, (rest - mid.astype(F32)).astype(BF16)


CHUNKS = ((0, 256), (256, 512), (768, 512), (1280, 512), (1792, 256))


def update_kernel(
    owned,
    given,
    mine,
    other,
    *refs,
):
    pairs, refs = refs[:3], refs[3:]
    trailing, updated, block, multipliers, swapped, own, columns, arrive, leave, sem = refs
    me = lax.axis_index("prow")

    def load(k):
        cols = pl.ds(*CHUNKS[k])
        return pltpu.make_async_copy(trailing.at[:, cols], block.at[:, cols], arrive.at[k])

    def store(k):
        cols = pl.ds(*CHUNKS[k])
        return pltpu.make_async_copy(block.at[:, cols], updated.at[:, cols], leave.at[k])

    copy = pltpu.make_async_copy(owned, own, sem)
    copy.start()
    for k in range(len(CHUNKS)):
        load(k).start()

    c = lax.axis_index("pcol")
    z, core = c // 2, c % 2

    def place(step, side, values):
        high, low = halves(values.T)
        start = (((z + step) & 3) * 2 + ((core + side) & 1)) * LANES
        rows = pl.ds(pl.multiple_of(start, LANES), LANES)
        multipliers[rows, :] = jnp.concatenate([high, low, high, low], axis=1)

    for side, panel in enumerate((mine, other)):
        place(0, side, panel[...])
        for step, pair in enumerate(pairs, 1):
            place(step, side, pair[side * NB : (side + 1) * NB, :])

    lower = unfold(given[NB:BACK, :])
    for j in range(NB):
        columns[j] = jnp.broadcast_to(lower[:, j : j + 1], (NB, LANES))

    row_id = lax.broadcasted_iota(jnp.int32, (8, LANES), 0)
    col_id = lax.broadcasted_iota(jnp.int32, (8, LANES), 1)
    inverse = [jnp.where(col_id == row_id + 8 * b, 1.0, 0.0).astype(F32) for b in range(8)]
    for j in range(NB):
        b, s = j // 8, j % 8
        row = jnp.broadcast_to(inverse[b][s : s + 1, :], (8, LANES))
        for i in range(b, 8):
            inverse[i] = inverse[i] - columns[j, 8 * i : 8 * i + 8, :] * row
    inv_high, inv_mid, inv_low = thirds(jnp.concatenate(inverse, axis=0)[:, 0:NB])
    left = jnp.concatenate([inv_high, inv_mid, inv_low, inv_high, inv_mid, inv_high], axis=1)

    copy.wait()
    n_own = own[0, 0]
    n_away = jnp.where(me == 0, 0, n_own)
    n_here = n_own - n_away

    def group_of(row):
        return pl.ds(pl.multiple_of(row // 8 * 8, 8), 8), row_id == row % 8

    def row_of(ref, row, part):
        group, here = group_of(row)
        return jnp.sum(jnp.where(here, ref[group, part], 0.0), axis=0, keepdims=True)

    for k, (start, width) in enumerate(CHUNKS):
        cols = slice(start, start + width)
        pieces = range(start // LANES, (start + width) // LANES)
        parts = [slice(p * LANES, (p + 1) * LANES) for p in pieces]
        load(k).wait()
        for n, p in enumerate(pieces):
            swapped[n * NB : (n + 1) * NB, :] = given[p * BACK : p * BACK + NB, :]

        def fetch(i, carry):
            row, j = own[0, 1 + i] // NB, own[0, 1 + i] % NB
            for n, part in enumerate(parts):
                swapped[pl.ds(n * NB + j, 1), :] = row_of(block, row, part)
            return carry

        lax.fori_loop(0, n_away, fetch, 0)
        tops = jnp.concatenate([swapped[n * NB : (n + 1) * NB, :] for n in range(len(parts))], axis=1)
        high, mid, low = thirds(tops)
        right = jnp.concatenate([high, high, high, mid, mid, low], axis=0)
        upper = jnp.dot(left, right, preferred_element_type=F32)
        up_high, up_low = halves(upper)
        factor = jnp.concatenate([up_high, up_high, up_low, up_low], axis=0)
        product = jnp.dot(multipliers[...], factor, preferred_element_type=F32)

        def displace(i, carry):
            row, j = own[0, 1 + i] // NB, own[0, 1 + i] % NB
            group, here = group_of(row)
            for p, part in zip(pieces, parts):
                moved = given[pl.ds(p * BACK + j, 1), :]
                block[group, part] = jnp.where(here, moved, block[group, part])
            return carry

        def displace_here(i, carry):
            row, t = own[0, 1 + i] // NB, own[0, 1 + i] % NB
            group, here = group_of(row)
            for part in parts:
                moved = row_of(block, t, part)
                block[group, part] = jnp.where(here, moved, block[group, part])
            return carry

        lax.fori_loop(0, n_away, displace, 0)
        lax.fori_loop(0, n_here, displace_here, 0)
        block[:, cols] = block[:, cols] - product

        @pl.when(me == 0)
        def _():
            block[0:NB, cols] = upper

        store(k).start()
    for k in range(len(CHUNKS)):
        store(k).wait()


def update(owned, given, panels, trailing):
    rows, cols = trailing.shape
    return pl.pallas_call(
        update_kernel,
        out_shape=jax.ShapeDtypeStruct((rows, cols), F32),
        in_specs=[VMEM] * 7 + [HBM],
        out_specs=HBM,
        scratch_shapes=[
            pltpu.VMEM((rows, cols), F32),
            pltpu.VMEM((rows, 4 * NB), BF16),
            pltpu.VMEM((4 * NB, LANES), F32),
            pltpu.SMEM((1, OWN), jnp.int32),
            pltpu.VMEM((NB, NB, LANES), F32),
            pltpu.SemaphoreType.DMA((len(CHUNKS),)),
            pltpu.SemaphoreType.DMA((len(CHUNKS),)),
            pltpu.SemaphoreType.DMA,
        ],
        compiler_params=pltpu.CompilerParams(vmem_limit_bytes=48 * 2**20),
    )(owned, given, *panels, trailing)


def ring(step):
    return [(c, (c // 2 + step) % 4 * 2 + c % 2) for c in range(N_PCOL)]


def body(trailing, factors, pivots):
    partner = lax.ppermute(factors, "pcol", [(c, c ^ 1) for c in range(N_PCOL)])
    sent = pick(pivots, trailing)
    pair = join(factors, partner)
    got = lax.all_to_all(sent, "prow", 0, 0)
    panels = [factors, partner] + [lax.ppermute(pair, "pcol", ring(4 - turn)) for turn in (1, 2, 3)]
    routes, owned = route(pivots)
    back = spread(routes, got.reshape(N_PROW * NB, LANES), panels)
    given = lax.all_to_all(back.reshape(N_PROW, BACK, LANES), "prow", 0, 0)
    return update(owned, given.reshape(N_PROW * BACK, LANES), panels, trailing)


def solution(mesh):
    return jax.shard_map(
        body,
        mesh=mesh,
        in_specs=(P("prow", "pcol"), P(None, ("prow", "pcol")), P()),
        out_specs=P("prow", "pcol"),
        check_vma=False,
    )
```

time: 50.5 us -> 48.8 us (0.966)
  blocking collectives: 0 us -> 18.3 us
  waiting for transfers between devices: 14.9 us -> 2.69 us
  starting transfers between devices: 18.6 us -> 12.8 us
  Pallas kernels: 15.4 us -> 14.3 us
  between operations: 0.9 us -> 0.06 us
    all_to_all x0 -> x1, blocking collectives: none -> 18.3 us  [body(): given = lax.all_to_all(back.reshape(N_PROW, BACK, LANES), 'prow', 0, 0)]
    all_to_all x2 -> x1, waiting for transfers between devices: 12.3 us -> 0.42 us  [body(): got = lax.all_to_all(sent, 'prow', 0, 0)]
    all_to_all x2 -> x1, starting transfers between devices: 12.6 us -> 6.19 us  [body(): got = lax.all_to_all(sent, 'prow', 0, 0)]
    pallas_call x5 -> x4, Pallas kernels: 15.4 us -> 14.3 us  [the longest x1 7.31 us: update(): pl.pallas_call(update_kernel, out_shape=jax.ShapeDtypeStruct((rows, cols)...]
    ppermute x3, starting transfers between devices: 5.9 us -> 6.51 us  [body(): lax.ppermute(pair, 'pcol', ring(4 - turn))]
  transfers between devices with their start and end apart: 6 -> 5, of which waited for: 4 -> 4; matrix products, arithmetic and copies ran while one was open for 0% -> 0% of each run, Pallas kernels for 9% -> 4%
where the time goes in v4:
time: 48.8 us; the launch traced here: 48.1 us
  blocking collectives  18.3 us (38%)
  Pallas kernels  14.3 us (29%)
  starting transfers between devices  12.8 us (26%)
  waiting for transfers between devices  2.69 us (6%)
    all_to_all x1, blocking collectives, body(): given = lax.all_to_all(back.reshape(N_PROW, BACK, LANES), 'prow', 0, 0)  18.3 us
    pallas_call x1, Pallas kernels, update(): pl.pallas_call(update_kernel, out_shape=jax.ShapeDtypeStruct((rows, cols)...  7.31 us
    ppermute x3, starting transfers between devices, body(): lax.ppermute(pair, 'pcol', ring(4 - turn))  6.51 us
    all_to_all x1, starting transfers between devices, body(): got = lax.all_to_all(sent, 'prow', 0, 0)  6.19 us
    pallas_call x1, Pallas kernels, pick(): pl.pallas_call(pick_kernel, out_shape=jax.ShapeDtypeStruct((N_PROW, NB, L...  4.11 us
    pallas_call x1, Pallas kernels, route(): pl.pallas_call(route_kernel, out_shape=(jax.ShapeDtypeStruct((1, ROUTES),...  2.16 us
    ppermute x1, waiting for transfers between devices, body(): partner = lax.ppermute(factors, 'pcol', [(c, c ^ 1) for c in range(N_PCOL)])  1.19 us
    ppermute x3, waiting for transfers between devices, body(): lax.ppermute(pair, 'pcol', ring(4 - turn))  1.08 us
  transfers between devices with their start and end apart: 5, of which 4 were waited for; matrix products, arithmetic and copies ran while one was open for 0% of the time, Pallas kernels for 4%

profile of v4, /device:TPU:0, one launch (start us, length us, event | category | flops | bytes accessed | tf_op | source)
XLA Modules:
  0.0 48.1 jit_solution(15045899438169206863)
XLA Ops:
  0.0 0.0 copy-start.1
  0.0 0.0 copy-start
  0.0 4.1 %shard_map.38 = f32[16,64,128]{2,1,0:T(8,128)} custom-call(s32[64]{0:T(128)} %pivots.3, f32[1024,2048]{1,0:T(8,128)} %refs_3_.1), custom_call_target="tpu_custom_call" | custom-call | tf_op jit(solution)/shard_map/pallas_call | solution.py:102
  4.1 6.2 %all-to-all-start = ((f32[16,64,128]{2,1,0:T(8,128)}), f32[16,64,128]{2,1,0:T(8,128)S(1)}, u32[]{:S(2)}, u32[]{:S(2)}) async-start(f32[16,64,128]{2,1,0:T(8,128)} %shard_map.38), calls=%async_computation | async-start | bytes 1048576 | tf_op jit(solution)/shard_map/all_to_all | solution.py:424
  10.3 0.0 copy-done
  10.3 0.1 collective-permute-start
  10.4 1.2 %collective-permute-done.other.refs_1_ = f32[64,128]{1,0:T(8,128)S(1)} collective-permute-done((f32[64,128]{1,0:T(8,128)S(1)}, f32[64,128]{1,0:T(8,128)S(1)}, u32[]{:S(2)}, u32[]{:S(2)}) %collective-permute-start) | collective-permute-done | bytes 32800 | tf_op jit(solution)/shard_map/ppermute | solution.py:421
  11.6 1.9 %collective-permute-start.3 = (f32[128,128]{1,0:T(8,128)S(1)}, f32[128,128]{1,0:T(8,128)S(1)}, u32[]{:S(2)}, u32[]{:S(2)}) collective-permute-start(f32[128,128]{1,0:T(8,128)S(1)} %shard_map.39), channel_id=1, source_target_pairs={{0,2},{1,3},{2,4},{3,5},{4,6},{5,7},{6,0},{7,1},{8,10},{9,11},{10,... | collective-permute-start | bytes 196616 | tf_op jit(solution)/shard_map/ppermute | solution.py:425
  13.5 3.6 %collective-permute-start.2 = (f32[128,128]{1,0:T(8,128)S(1)}, f32[128,128]{1,0:T(8,128)S(1)}, u32[]{:S(2)}, u32[]{:S(2)}) collective-permute-start(f32[128,128]{1,0:T(8,128)S(1)} %shard_map.39), channel_id=1, source_target_pairs={{0,4},{1,5},{2,6},{3,7},{4,0},{5,1},{6,2},{7,3},{8,12},{9,13},{10,... | collective-permute-start | bytes 196616 | tf_op jit(solution)/shard_map/ppermute | solution.py:425
  17.1 1.0 %collective-permute-start.1 = (f32[128,128]{1,0:T(8,128)S(1)}, f32[128,128]{1,0:T(8,128)S(1)}, u32[]{:S(2)}, u32[]{:S(2)}) collective-permute-start(f32[128,128]{1,0:T(8,128)S(1)} %shard_map.39), channel_id=1, source_target_pairs={{0,6},{1,7},{2,0},{3,1},{4,2},{5,3},{6,4},{7,5},{8,14},{9,15},{10,... | collective-permute-start | bytes 196616 | tf_op jit(solution)/shard_map/ppermute | solution.py:425
  18.1 0.0 copy-done.1
  18.1 2.2 %shard_map.37 = (s32[1,192]{1,0:T(1,128)S(1)}, s32[1,128]{1,0:T(1,128)S(1)}) custom-call(s32[64]{0:T(128)S(1)} %copy-done.1), custom_call_target="tpu_custom_call" | custom-call | tf_op jit(solution)/shard_map/pallas_call | solution.py:171
  20.3 0.0 collective-permute-done.3.refs_4_.refs_2_
  20.3 0.3 collective-permute-done.2.refs_3_.refs_1_
  20.7 0.7 %collective-permute-done.1.refs_2_.refs_0_ = f32[128,128]{1,0:T(8,128)S(1)} collective-permute-done((f32[128,128]{1,0:T(8,128)S(1)}, f32[128,128]{1,0:T(8,128)S(1)}, u32[]{:S(2)}, u32[]{:S(2)}) %collective-permute-start.1) | collective-permute-done | bytes 65568 | tf_op jit(solution)/shard_map/ppermute | solution.py:425
  21.4 0.4 all-to-all-done
  21.8 0.7 %shard_map.40 = f32[1280,128]{1,0:T(8,128)S(1)} custom-call(s32[1,192]{1,0:T(1,128)S(1)} %get-tuple-element.8.routes, f32[1024,128]{1,0:T(8,128)S(1)} %bitcast.5, f32[64,128]{1,0:T(8,128)S(1)} %copy-done, f32[64,128]{1,0:T(8,128)S(1)} %collective-permute-done.other.refs_1_, f32[128,128]{1,0:T(8,128)S(1)} %collective-permute-done.1.refs_2_.refs_0_, ...), custom_call_target="tpu_custom_call" | custom-call | tf_op jit(solution)/shard_map/pallas_call | solution.py:249
  22.5 18.3 %all_to_all.10 = f32[16,80,128]{2,1,0:T(8,128)S(1)} all-to-all(f32[16,80,128]{2,1,0:T(8,128)S(1)} %bitcast.4), channel_id=1, replica_groups=mesh['prow'=16,'pcol'=8] {'prow'}, dimensions={0} | all-to-all | bytes 1310720 | tf_op jit(solution)/shard_map/all_to_all | solution.py:428
  40.8 7.3 %shard_map.41 = f32[1024,2048]{1,0:T(8,128)} custom-call(s32[1,128]{1,0:T(1,128)S(1)} %get-tuple-element.7.owned, f32[1280,128]{1,0:T(8,128)S(1)} %bitcast.3, f32[64,128]{1,0:T(8,128)S(1)} %copy-done, f32[64,128]{1,0:T(8,128)S(1)} %collective-permute-done.other.refs_1_, f32[128,128]{1,0:T(8,128)S(1)} %collective-permute-done.1.refs_2_.refs_0_, ...), custom_call_target="tpu_custom_call" | custom-call | tf_op jit(solution)/shard_map/pallas_call | solution.py:397
  (1 shorter events, 0.0 us)
Async XLA Ops:
  0.0 18.1 %copy-start.1 = (s32[64]{0:T(128)S(1)}, s32[64]{0:T(128)}, u32[]{:S(2)}) copy-start(s32[64]{0:T(128)} %pivots.3) | copy-start | bytes 772
  0.0 10.3 %copy-start = (f32[64,128]{1,0:T(8,128)S(1)}, f32[64,128]{1,0:T(8,128)}, u32[]{:S(2)}) copy-start(f32[64,128]{1,0:T(8,128)} %mine.3) | copy-start | bytes 98308
  4.1 17.7 %all-to-all-start = ((f32[16,64,128]{2,1,0:T(8,128)}), f32[16,64,128]{2,1,0:T(8,128)S(1)}, u32[]{:S(2)}, u32[]{:S(2)}) async-start(f32[16,64,128]{2,1,0:T(8,128)} %shard_map.38), calls=%async_computation | async-start | bytes 1048576 | tf_op jit(solution)/shard_map/all_to_all | solution.py:424
  10.3 1.3 %collective-permute-start = (f32[64,128]{1,0:T(8,128)S(1)}, f32[64,128]{1,0:T(8,128)S(1)}, u32[]{:S(2)}, u32[]{:S(2)}) collective-permute-start(f32[64,128]{1,0:T(8,128)S(1)} %copy-done), channel_id=1, source_target_pairs={{0,1},{1,0},{2,3},{3,2},{4,5},{5,4},{6,7},{7,6},{8,9},{9,8},{10,11... | collective-permute-start | bytes 98312 | tf_op jit(solution)/shard_map/ppermute | solution.py:421
  11.6 8.7 %collective-permute-start.3 = (f32[128,128]{1,0:T(8,128)S(1)}, f32[128,128]{1,0:T(8,128)S(1)}, u32[]{:S(2)}, u32[]{:S(2)}) collective-permute-start(f32[128,128]{1,0:T(8,128)S(1)} %shard_map.39), channel_id=1, source_target_pairs={{0,2},{1,3},{2,4},{3,5},{4,6},{5,7},{6,0},{7,1},{8,10},{9,11},{10,... | collective-permute-start | bytes 196616 | tf_op jit(solution)/shard_map/ppermute | solution.py:425
  13.5 7.1 %collective-permute-start.2 = (f32[128,128]{1,0:T(8,128)S(1)}, f32[128,128]{1,0:T(8,128)S(1)}, u32[]{:S(2)}, u32[]{:S(2)}) collective-permute-start(f32[128,128]{1,0:T(8,128)S(1)} %shard_map.39), channel_id=1, source_target_pairs={{0,4},{1,5},{2,6},{3,7},{4,0},{5,1},{6,2},{7,3},{8,12},{9,13},{10,... | collective-permute-start | bytes 196616 | tf_op jit(solution)/shard_map/ppermute | solution.py:425
  17.1 4.3 %collective-permute-start.1 = (f32[128,128]{1,0:T(8,128)S(1)}, f32[128,128]{1,0:T(8,128)S(1)}, u32[]{:S(2)}, u32[]{:S(2)}) collective-permute-start(f32[128,128]{1,0:T(8,128)S(1)} %shard_map.39), channel_id=1, source_target_pairs={{0,6},{1,7},{2,0},{3,1},{4,2},{5,3},{6,4},{7,5},{8,14},{9,15},{10,... | collective-permute-start | bytes 196616 | tf_op jit(solution)/shard_map/ppermute | solution.py:425

commit v5 on v4

--- a/solution.py
+++ b/solution.py
@@ -283,7 +283,8 @@
     *refs,
 ):
     pairs, refs = refs[:3], refs[3:]
-    trailing, updated, block, multipliers, swapped, own, columns, arrive, leave, sem = refs
+    trailing, updated, block, kept, chosen, tops_here, multipliers, own, columns = refs[:9]
+    arrive, leave, sem, row_sem = refs[9:]
     me = lax.axis_index("prow")
 
     def load(k):
@@ -296,7 +297,36 @@
 
     copy = pltpu.make_async_copy(owned, own, sem)
     copy.start()
-    for k in range(len(CHUNKS)):
+    load(0).start()
+
+    copy.wait()
+    n_own = own[0, 0]
+    n_away = jnp.where(me == 0, 0, n_own)
+    n_here = n_own - n_away
+
+    row_id = lax.broadcasted_iota(jnp.int32, (8, LANES), 0)
+
+    def group_of(row):
+        return pl.ds(pl.multiple_of(row // 8 * 8, 8), 8), row_id == row % 8
+
+    def row_copy(i):
+        row, j = own[0, 1 + i] // NB, own[0, 1 + i] % NB
+        return pltpu.make_async_copy(
+            trailing.at[pl.ds(row, 1), :], kept.at[pl.ds(j, 1), :], row_sem
+        )
+
+    def fetch(i, carry):
+        row_copy(i).start()
+        chosen[pl.ds(own[0, 1 + i] % NB, 1), :] = jnp.ones((1, LANES), F32)
+        return carry
+
+    def fetched(i, carry):
+        row_copy(i).wait()
+        return carry
+
+    chosen[...] = jnp.zeros_like(chosen)
+    lax.fori_loop(0, n_away, fetch, 0)
+    for k in range(1, len(CHUNKS)):
         load(k).start()
 
     c = lax.axis_index("pcol")
@@ -328,34 +358,19 @@
     inv_high, inv_mid, inv_low = thirds(jnp.concatenate(inverse, axis=0)[:, 0:NB])
     left = jnp.concatenate([inv_high, inv_mid, inv_low, inv_high, inv_mid, inv_high], axis=1)
 
-    copy.wait()
-    n_own = own[0, 0]
-    n_away = jnp.where(me == 0, 0, n_own)
-    n_here = n_own - n_away
-
-    def group_of(row):
-        return pl.ds(pl.multiple_of(row // 8 * 8, 8), 8), row_id == row % 8
-
-    def row_of(ref, row, part):
-        group, here = group_of(row)
-        return jnp.sum(jnp.where(here, ref[group, part], 0.0), axis=0, keepdims=True)
-
+    lax.fori_loop(0, n_away, fetched, 0)
     for k, (start, width) in enumerate(CHUNKS):
         cols = slice(start, start + width)
         pieces = range(start // LANES, (start + width) // LANES)
         parts = [slice(p * LANES, (p + 1) * LANES) for p in pieces]
         load(k).wait()
-        for n, p in enumerate(pieces):
-            swapped[n * NB : (n + 1) * NB, :] = given[p * BACK : p * BACK + NB, :]
-
-        def fetch(i, carry):
-            row, j = own[0, 1 + i] // NB, own[0, 1 + i] % NB
-            for n, part in enumerate(parts):
-                swapped[pl.ds(n * NB + j, 1), :] = row_of(block, row, part)
-            return carry
-
-        lax.fori_loop(0, n_away, fetch, 0)
-        tops = jnp.concatenate([swapped[n * NB : (n + 1) * NB, :] for n in range(len(parts))], axis=1)
+        tops = jnp.concatenate(
+            [
+                jnp.where(chosen[...] > 0, kept[:, part], given[p * BACK : p * BACK + NB, :])
+                for p, part in zip(pieces, parts)
+            ],
+            axis=1,
+        )
         high, mid, low = thirds(tops)
         right = jnp.concatenate([high, high, high, mid, mid, low], axis=0)
         upper = jnp.dot(left, right, preferred_element_type=F32)
@@ -374,10 +389,15 @@
         def displace_here(i, carry):
             row, t = own[0, 1 + i] // NB, own[0, 1 + i] % NB
             group, here = group_of(row)
-            for part in parts:
-                moved = row_of(block, t, part)
+            for n, part in enumerate(parts):
+                moved = tops_here[pl.ds(n * NB + t, 1), :]
                 block[group, part] = jnp.where(here, moved, block[group, part])
             return carry
+
+        @pl.when(me == 0)
+        def _():
+            for n, part in enumerate(parts):
+                tops_here[n * NB : (n + 1) * NB, :] = block[0:NB, part]
 
         lax.fori_loop(0, n_away, displace, 0)
         lax.fori_loop(0, n_here, displace_here, 0)
@@ -401,13 +421,16 @@
         out_specs=HBM,
         scratch_shapes=[
             pltpu.VMEM((rows, cols), F32),
+            pltpu.VMEM((NB, cols), F32),
+            pltpu.VMEM((NB, LANES), F32),
+            pltpu.VMEM((4 * NB, LANES), F32),
             pltpu.VMEM((rows, 4 * NB), BF16),
-            pltpu.VMEM((4 * NB, LANES), F32),
             pltpu.SMEM((1, OWN), jnp.int32),
             pltpu.VMEM((NB, NB, LANES), F32),
             pltpu.SemaphoreType.DMA((len(CHUNKS),)),
             pltpu.SemaphoreType.DMA((len(CHUNKS),)),
             pltpu.SemaphoreType.DMA,
+            pltpu.SemaphoreType.DMA,
         ],
         compiler_params=pltpu.CompilerParams(vmem_limit_bytes=48 * 2**20),
     )(owned, given, *panels, trailing)
@@ -419,7 +442,7 @@
 
 def body(trailing, factors, pivots):
     partner = lax.ppermute(factors, "pcol", [(c, c ^ 1) for c in range(N_PCOL)])
-    sent = pick(pivots, trailing)
+    sent, partner = lax.optimization_barrier((pick(pivots, trailing), partner))
     pair = join(factors, partner)
     got = lax.all_to_all(sent, "prow", 0, 0)
     panels = [factors, partner] + [lax.ppermute(pair, "pcol", ring(4 - turn)) for turn in (1, 2, 3)]

time: 48.8 us -> 47.1 us (0.965)
  blocking collectives: 18.3 us -> 16.2 us
  waiting for transfers between devices: 2.69 us -> 3.23 us
    all_to_all x1, blocking collectives: 18.3 us -> 16.2 us  [body(): given = lax.all_to_all(back.reshape(N_PROW, BACK, LANES), 'prow', 0, 0)]
    all_to_all x1, waiting for transfers between devices: 0.42 us -> 2.14 us  [body(): got = lax.all_to_all(sent, 'prow', 0, 0)]
    ppermute x1, waiting for transfers between devices: 1.19 us -> 0.01 us  [body(): partner = lax.ppermute(factors, 'pcol', [(c, c ^ 1) for c in range(N_PCOL)])]
  transfers between devices with their start and end apart: 5 -> 5, of which waited for: 4 -> 3; matrix products, arithmetic and copies ran while one was open for 0% -> 0% of each run, Pallas kernels for 4% -> 13%
where the time goes in v5:
time: 47.1 us; the launch traced here: 46.4 us
  blocking collectives  16.2 us (34%)
  Pallas kernels  14.2 us (30%)
  starting transfers between devices  12.8 us (27%)
  waiting for transfers between devices  3.23 us (7%)
    all_to_all x1, blocking collectives, body(): given = lax.all_to_all(back.reshape(N_PROW, BACK, LANES), 'prow', 0, 0)  16.2 us
    pallas_call x1, Pallas kernels, update(): pl.pallas_call(update_kernel, out_shape=jax.ShapeDtypeStruct((rows, cols)...  7.29 us
    ppermute x3, starting transfers between devices, body(): lax.ppermute(pair, 'pcol', ring(4 - turn))  6.58 us
    all_to_all x1, starting transfers between devices, body(): got = lax.all_to_all(sent, 'prow', 0, 0)  6.21 us
    pallas_call x1, Pallas kernels, pick(): pl.pallas_call(pick_kernel, out_shape=jax.ShapeDtypeStruct((N_PROW, NB, L...  4.05 us
    pallas_call x1, Pallas kernels, route(): pl.pallas_call(route_kernel, out_shape=(jax.ShapeDtypeStruct((1, ROUTES),...  2.16 us
    all_to_all x1, waiting for transfers between devices, body(): got = lax.all_to_all(sent, 'prow', 0, 0)  2.14 us
    ppermute x3, waiting for transfers between devices, body(): lax.ppermute(pair, 'pcol', ring(4 - turn))  1.08 us
  transfers between devices with their start and end apart: 5, of which 3 were waited for; matrix products, arithmetic and copies ran while one was open for 0% of the time, Pallas kernels for 13%

profile of v5, /device:TPU:0, one launch (start us, length us, event | category | flops | bytes accessed | tf_op | source)
XLA Modules:
  0.0 46.4 jit_solution(8194770407309118670)
XLA Ops:
  0.0 0.0 copy-start
  0.0 0.0 copy-start.1
  0.0 0.0 collective-permute-start
  0.0 4.1 %shard_map.38 = f32[16,64,128]{2,1,0:T(8,128)} custom-call(s32[64]{0:T(128)} %pivots.3, f32[1024,2048]{1,0:T(8,128)} %refs_3_.1), custom_call_target="tpu_custom_call" | custom-call | tf_op jit(solution)/shard_map/pallas_call | solution.py:102
  4.1 0.0 collective-permute-done.other.refs_1_
  4.1 6.2 %all-to-all-start = ((f32[16,64,128]{2,1,0:T(8,128)}), f32[16,64,128]{2,1,0:T(8,128)S(1)}, u32[]{:S(2)}, u32[]{:S(2)}) async-start(f32[16,64,128]{2,1,0:T(8,128)} %shard_map.38), calls=%async_computation | async-start | bytes 1048576 | tf_op jit(solution)/shard_map/all_to_all | solution.py:447
  10.3 0.0 copy-done
  10.3 2.0 %collective-permute-start.3 = (f32[128,128]{1,0:T(8,128)S(1)}, f32[128,128]{1,0:T(8,128)S(1)}, u32[]{:S(2)}, u32[]{:S(2)}) collective-permute-start(f32[128,128]{1,0:T(8,128)S(1)} %shard_map.39), channel_id=1, source_target_pairs={{0,2},{1,3},{2,4},{3,5},{4,6},{5,7},{6,0},{7,1},{8,10},{9,11},{10,... | collective-permute-start | bytes 196616 | tf_op jit(solution)/shard_map/ppermute | solution.py:448
  12.3 3.6 %collective-permute-start.2 = (f32[128,128]{1,0:T(8,128)S(1)}, f32[128,128]{1,0:T(8,128)S(1)}, u32[]{:S(2)}, u32[]{:S(2)}) collective-permute-start(f32[128,128]{1,0:T(8,128)S(1)} %shard_map.39), channel_id=1, source_target_pairs={{0,4},{1,5},{2,6},{3,7},{4,0},{5,1},{6,2},{7,3},{8,12},{9,13},{10,... | collective-permute-start | bytes 196616 | tf_op jit(solution)/shard_map/ppermute | solution.py:448
  15.9 1.0 %collective-permute-start.1 = (f32[128,128]{1,0:T(8,128)S(1)}, f32[128,128]{1,0:T(8,128)S(1)}, u32[]{:S(2)}, u32[]{:S(2)}) collective-permute-start(f32[128,128]{1,0:T(8,128)S(1)} %shard_map.39), channel_id=1, source_target_pairs={{0,6},{1,7},{2,0},{3,1},{4,2},{5,3},{6,4},{7,5},{8,14},{9,15},{10,... | collective-permute-start | bytes 196616 | tf_op jit(solution)/shard_map/ppermute | solution.py:448
  16.9 0.0 copy-done.1
  16.9 2.2 %shard_map.37 = (s32[1,192]{1,0:T(1,128)S(1)}, s32[1,128]{1,0:T(1,128)S(1)}) custom-call(s32[64]{0:T(128)S(1)} %copy-done.1), custom_call_target="tpu_custom_call" | custom-call | tf_op jit(solution)/shard_map/pallas_call | solution.py:171
  19.1 0.0 collective-permute-done.3.refs_4_.refs_2_
  19.1 0.3 collective-permute-done.2.refs_3_.refs_1_
  19.3 0.8 %collective-permute-done.1.refs_2_.refs_0_ = f32[128,128]{1,0:T(8,128)S(1)} collective-permute-done((f32[128,128]{1,0:T(8,128)S(1)}, f32[128,128]{1,0:T(8,128)S(1)}, u32[]{:S(2)}, u32[]{:S(2)}) %collective-permute-start.1) | collective-permute-done | bytes 65568 | tf_op jit(solution)/shard_map/ppermute | solution.py:448
  20.2 2.1 %all-to-all-done = f32[16,64,128]{2,1,0:T(8,128)S(1)} async-done(((f32[16,64,128]{2,1,0:T(8,128)}), f32[16,64,128]{2,1,0:T(8,128)S(1)}, u32[]{:S(2)}, u32[]{:S(2)}) %all-to-all-start) | async-done | bytes 524320 | tf_op jit(solution)/shard_map/all_to_all | solution.py:447
  22.3 0.7 %shard_map.40 = f32[1280,128]{1,0:T(8,128)S(1)} custom-call(s32[1,192]{1,0:T(1,128)S(1)} %get-tuple-element.10.routes, f32[1024,128]{1,0:T(8,128)S(1)} %bitcast.5, f32[64,128]{1,0:T(8,128)S(1)} %copy-done, f32[64,128]{1,0:T(8,128)S(1)} %collective-permute-done.other.refs_1_, f32[128,128]{1,0:T(8,128)S(1)} %collective-permute-done.1.refs_2_.refs_0_, ...), custom_call_target="tpu_custom_call" | custom-call | tf_op jit(solution)/shard_map/pallas_call | solution.py:249
  23.0 16.2 %all_to_all.10 = f32[16,80,128]{2,1,0:T(8,128)S(1)} all-to-all(f32[16,80,128]{2,1,0:T(8,128)S(1)} %bitcast.4), channel_id=1, replica_groups=mesh['prow'=16,'pcol'=8] {'prow'}, dimensions={0} | all-to-all | bytes 1310720 | tf_op jit(solution)/shard_map/all_to_all | solution.py:451
  39.1 7.3 %shard_map.41 = f32[1024,2048]{1,0:T(8,128)} custom-call(s32[1,128]{1,0:T(1,128)S(1)} %get-tuple-element.9.owned, f32[1280,128]{1,0:T(8,128)S(1)} %bitcast.3, f32[64,128]{1,0:T(8,128)S(1)} %copy-done, f32[64,128]{1,0:T(8,128)S(1)} %collective-permute-done.other.refs_1_, f32[128,128]{1,0:T(8,128)S(1)} %collective-permute-done.1.refs_2_.refs_0_, ...), custom_call_target="tpu_custom_call" | custom-call | tf_op jit(solution)/shard_map/pallas_call | solution.py:417
  (1 shorter events, 0.0 us)
Async XLA Ops:
  0.0 10.3 %copy-start = (f32[64,128]{1,0:T(8,128)S(1)}, f32[64,128]{1,0:T(8,128)}, u32[]{:S(2)}) copy-start(f32[64,128]{1,0:T(8,128)} %mine.3) | copy-start | bytes 98308
  0.0 16.9 %copy-start.1 = (s32[64]{0:T(128)S(1)}, s32[64]{0:T(128)}, u32[]{:S(2)}) copy-start(s32[64]{0:T(128)} %pivots.3) | copy-start | bytes 772
  0.0 4.1 %collective-permute-start = (f32[64,128]{1,0:T(8,128)}, f32[64,128]{1,0:T(8,128)S(1)}, u32[]{:S(2)}, u32[]{:S(2)}) collective-permute-start(f32[64,128]{1,0:T(8,128)} %mine.3), channel_id=1, source_target_pairs={{0,1},{1,0},{2,3},{3,2},{4,5},{5,4},{6,7},{7,6},{8,9},{9,8},{10,11... | collective-permute-start | bytes 98312 | tf_op jit(solution)/shard_map/ppermute | solution.py:444
  4.1 18.2 %all-to-all-start = ((f32[16,64,128]{2,1,0:T(8,128)}), f32[16,64,128]{2,1,0:T(8,128)S(1)}, u32[]{:S(2)}, u32[]{:S(2)}) async-start(f32[16,64,128]{2,1,0:T(8,128)} %shard_map.38), calls=%async_computation | async-start | bytes 1048576 | tf_op jit(solution)/shard_map/all_to_all | solution.py:447
  10.3 8.8 %collective-permute-start.3 = (f32[128,128]{1,0:T(8,128)S(1)}, f32[128,128]{1,0:T(8,128)S(1)}, u32[]{:S(2)}, u32[]{:S(2)}) collective-permute-start(f32[128,128]{1,0:T(8,128)S(1)} %shard_map.39), channel_id=1, source_target_pairs={{0,2},{1,3},{2,4},{3,5},{4,6},{5,7},{6,0},{7,1},{8,10},{9,11},{10,... | collective-permute-start | bytes 196616 | tf_op jit(solution)/shard_map/ppermute | solution.py:448
  12.3 7.0 %collective-permute-start.2 = (f32[128,128]{1,0:T(8,128)S(1)}, f32[128,128]{1,0:T(8,128)S(1)}, u32[]{:S(2)}, u32[]{:S(2)}) collective-permute-start(f32[128,128]{1,0:T(8,128)S(1)} %shard_map.39), channel_id=1, source_target_pairs={{0,4},{1,5},{2,6},{3,7},{4,0},{5,1},{6,2},{7,3},{8,12},{9,13},{10,... | collective-permute-start | bytes 196616 | tf_op jit(solution)/shard_map/ppermute | solution.py:448
  15.9 4.3 %collective-permute-start.1 = (f32[128,128]{1,0:T(8,128)S(1)}, f32[128,128]{1,0:T(8,128)S(1)}, u32[]{:S(2)}, u32[]{:S(2)}) collective-permute-start(f32[128,128]{1,0:T(8,128)S(1)} %shard_map.39), channel_id=1, source_target_pairs={{0,6},{1,7},{2,0},{3,1},{4,2},{5,3},{6,4},{7,5},{8,14},{9,15},{10,... | collective-permute-start | bytes 196616 | tf_op jit(solution)/shard_map/ppermute | solution.py:448

commit v6 on v5

--- a/solution.py
+++ b/solution.py
@@ -36,13 +36,13 @@
         visit(j, row)
 
 
-def pick_kernel(pivots, trailing, sent, order, count, rows, slots, sem, top_sem):
+def pick_kernel(pivots, trailing, sent, order, count, rows, slots, apart, sem, top_sem):
     me = lax.axis_index("prow")
 
-    def row_copy(row, slot, piece):
+    def row_copy(row, slot, piece, target):
         return pltpu.make_async_copy(
             trailing.at[pl.ds(row, 1), pl.ds(piece * LANES, LANES)],
-            sent.at[piece, pl.ds(slot, 1), :],
+            target.at[piece, pl.ds(slot, 1), :],
             sem,
         )
 
@@ -70,26 +70,40 @@
     swap_chain(pivots, order, visit)
     n_mine = count[0]
 
+    n_apart = jnp.where(me == 0, n_mine, 0)
+
+    def send(i, carry):
+        for piece in range(N_PROW):
+            row_copy(local_of(rows[i]), slots[i], piece, sent).start()
+        return carry
+
+    def send_apart(i, carry):
+        for piece in range(N_PROW):
+            row_copy(local_of(rows[i]), i, piece, apart).start()
+        return carry
+
+    lax.fori_loop(0, n_mine - n_apart, send, 0)
+    lax.fori_loop(0, n_apart, send_apart, 0)
+
     @pl.when(me == 0)
     def _():
         for piece in range(N_PROW):
             top_copy(piece).wait()
 
-    def send(i, carry):
-        row = rows[i]
-        slot = jnp.where(me == 0, order[row], slots[i])
-        for piece in range(N_PROW):
-            row_copy(local_of(row), slot, piece).start()
-        return carry
-
-    lax.fori_loop(0, n_mine, send, 0)
-
     def finish(i, carry):
         for piece in range(N_PROW):
-            row_copy(0, 0, piece).wait()
+            row_copy(0, 0, piece, sent).wait()
         return carry
 
     lax.fori_loop(0, n_mine, finish, 0)
+
+    def replace(i, carry):
+        slot = order[rows[i]]
+        for piece in range(N_PROW):
+            sent[piece, pl.ds(slot, 1), :] = apart[piece, pl.ds(i, 1), :]
+        return carry
+
+    lax.fori_loop(0, n_apart, replace, 0)
 
 
 SMEM = pl.BlockSpec(memory_space=pltpu.SMEM)
@@ -109,6 +123,7 @@
             pltpu.SMEM((1,), jnp.int32),
             pltpu.SMEM((NB + 1,), jnp.int32),
             pltpu.SMEM((NB + 1,), jnp.int32),
+            pltpu.VMEM((N_PROW, NB, LANES), F32),
             pltpu.SemaphoreType.DMA,
             pltpu.SemaphoreType.DMA((N_PROW,)),
         ],
@@ -272,7 +287,7 @@
     return high, mid, (rest - mid.astype(F32)).astype(BF16)
 
 
-CHUNKS = ((0, 256), (256, 512), (768, 512), (1280, 512), (1792, 256))
+CHUNKS = ((0, 512), (512, 512), (1024, 512), (1536, 512))
 
 
 def update_kernel(
@@ -298,6 +313,7 @@
     copy = pltpu.make_async_copy(owned, own, sem)
     copy.start()
     load(0).start()
+    load(1).start()
 
     copy.wait()
     n_own = own[0, 0]
@@ -326,7 +342,7 @@
 
     chosen[...] = jnp.zeros_like(chosen)
     lax.fori_loop(0, n_away, fetch, 0)
-    for k in range(1, len(CHUNKS)):
+    for k in range(2, len(CHUNKS)):
         load(k).start()
 
     c = lax.axis_index("pcol")

time: 47.1 us -> 46.4 us (0.985)
  Pallas kernels: 14.2 us -> 12.7 us
  starting transfers between devices: 12.8 us -> 13.7 us
    all_to_all x1, starting transfers between devices: 6.21 us -> 7.11 us  [body(): got = lax.all_to_all(sent, 'prow', 0, 0)]
    pallas_call x1, Pallas kernels: 4.05 us -> 3.29 us  [pick(): pl.pallas_call(pick_kernel, out_shape=jax.ShapeDtypeStruct((N_PROW, NB, L...]
    pallas_call x1, Pallas kernels: 7.29 us -> 6.62 us  [update(): pl.pallas_call(update_kernel, out_shape=jax.ShapeDtypeStruct((rows, cols)...]
  transfers between devices with their start and end apart: 5 -> 5, of which waited for: 3 -> 3; matrix products, arithmetic and copies ran while one was open for 0% -> 0% of each run, Pallas kernels for 13% -> 12%
where the time goes in v6:
time: 46.4 us; the launch traced here: 45.9 us
  blocking collectives  16.2 us (35%)
  starting transfers between devices  13.7 us (30%)
  Pallas kernels  12.7 us (27%)
  waiting for transfers between devices  3.23 us (7%)
    all_to_all x1, blocking collectives, body(): given = lax.all_to_all(back.reshape(N_PROW, BACK, LANES), 'prow', 0, 0)  16.2 us
    all_to_all x1, starting transfers between devices, body(): got = lax.all_to_all(sent, 'prow', 0, 0)  7.11 us
    pallas_call x1, Pallas kernels, update(): pl.pallas_call(update_kernel, out_shape=jax.ShapeDtypeStruct((rows, cols)...  6.62 us
    ppermute x3, starting transfers between devices, body(): lax.ppermute(pair, 'pcol', ring(4 - turn))  6.58 us
    pallas_call x1, Pallas kernels, pick(): pl.pallas_call(pick_kernel, out_shape=jax.ShapeDtypeStruct((N_PROW, NB, L...  3.29 us
    pallas_call x1, Pallas kernels, route(): pl.pallas_call(route_kernel, out_shape=(jax.ShapeDtypeStruct((1, ROUTES),...  2.16 us
    all_to_all x1, waiting for transfers between devices, body(): got = lax.all_to_all(sent, 'prow', 0, 0)  2.14 us
    ppermute x3, waiting for transfers between devices, body(): lax.ppermute(pair, 'pcol', ring(4 - turn))  1.08 us
  transfers between devices with their start and end apart: 5, of which 3 were waited for; matrix products, arithmetic and copies ran while one was open for 0% of the time, Pallas kernels for 12%

profile of v6, /device:TPU:0, one launch (start us, length us, event | category | flops | bytes accessed | tf_op | source)
XLA Modules:
  0.0 45.9 jit_solution(18010533443962187364)
XLA Ops:
  0.0 0.0 copy-start
  0.0 0.0 copy-start.1
  0.0 0.0 collective-permute-start
  0.0 3.3 %shard_map.38 = f32[16,64,128]{2,1,0:T(8,128)} custom-call(s32[64]{0:T(128)} %pivots.3, f32[1024,2048]{1,0:T(8,128)} %refs_3_.1), custom_call_target="tpu_custom_call" | custom-call | tf_op jit(solution)/shard_map/pallas_call | solution.py:116
  3.3 0.0 collective-permute-done.other.refs_1_
  3.3 7.1 %all-to-all-start = ((f32[16,64,128]{2,1,0:T(8,128)}), f32[16,64,128]{2,1,0:T(8,128)S(1)}, u32[]{:S(2)}, u32[]{:S(2)}) async-start(f32[16,64,128]{2,1,0:T(8,128)} %shard_map.38), calls=%async_computation | async-start | bytes 1048576 | tf_op jit(solution)/shard_map/all_to_all | solution.py:463
  10.4 0.0 copy-done
  10.5 2.0 %collective-permute-start.3 = (f32[128,128]{1,0:T(8,128)S(1)}, f32[128,128]{1,0:T(8,128)S(1)}, u32[]{:S(2)}, u32[]{:S(2)}) collective-permute-start(f32[128,128]{1,0:T(8,128)S(1)} %shard_map.39), channel_id=1, source_target_pairs={{0,2},{1,3},{2,4},{3,5},{4,6},{5,7},{6,0},{7,1},{8,10},{9,11},{10,... | collective-permute-start | bytes 196616 | tf_op jit(solution)/shard_map/ppermute | solution.py:464
  12.4 3.6 %collective-permute-start.2 = (f32[128,128]{1,0:T(8,128)S(1)}, f32[128,128]{1,0:T(8,128)S(1)}, u32[]{:S(2)}, u32[]{:S(2)}) collective-permute-start(f32[128,128]{1,0:T(8,128)S(1)} %shard_map.39), channel_id=1, source_target_pairs={{0,4},{1,5},{2,6},{3,7},{4,0},{5,1},{6,2},{7,3},{8,12},{9,13},{10,... | collective-permute-start | bytes 196616 | tf_op jit(solution)/shard_map/ppermute | solution.py:464
  16.0 1.0 %collective-permute-start.1 = (f32[128,128]{1,0:T(8,128)S(1)}, f32[128,128]{1,0:T(8,128)S(1)}, u32[]{:S(2)}, u32[]{:S(2)}) collective-permute-start(f32[128,128]{1,0:T(8,128)S(1)} %shard_map.39), channel_id=1, source_target_pairs={{0,6},{1,7},{2,0},{3,1},{4,2},{5,3},{6,4},{7,5},{8,14},{9,15},{10,... | collective-permute-start | bytes 196616 | tf_op jit(solution)/shard_map/ppermute | solution.py:464
  17.0 0.0 copy-done.1
  17.0 2.2 %shard_map.37 = (s32[1,192]{1,0:T(1,128)S(1)}, s32[1,128]{1,0:T(1,128)S(1)}) custom-call(s32[64]{0:T(128)S(1)} %copy-done.1), custom_call_target="tpu_custom_call" | custom-call | tf_op jit(solution)/shard_map/pallas_call | solution.py:186
  19.2 0.0 collective-permute-done.3.refs_4_.refs_2_
  19.2 0.3 collective-permute-done.2.refs_3_.refs_1_
  19.5 0.8 %collective-permute-done.1.refs_2_.refs_0_ = f32[128,128]{1,0:T(8,128)S(1)} collective-permute-done((f32[128,128]{1,0:T(8,128)S(1)}, f32[128,128]{1,0:T(8,128)S(1)}, u32[]{:S(2)}, u32[]{:S(2)}) %collective-permute-start.1) | collective-permute-done | bytes 65568 | tf_op jit(solution)/shard_map/ppermute | solution.py:464
  20.3 2.1 %all-to-all-done = f32[16,64,128]{2,1,0:T(8,128)S(1)} async-done(((f32[16,64,128]{2,1,0:T(8,128)}), f32[16,64,128]{2,1,0:T(8,128)S(1)}, u32[]{:S(2)}, u32[]{:S(2)}) %all-to-all-start) | async-done | bytes 524320 | tf_op jit(solution)/shard_map/all_to_all | solution.py:463
  22.4 0.7 %shard_map.40 = f32[1280,128]{1,0:T(8,128)S(1)} custom-call(s32[1,192]{1,0:T(1,128)S(1)} %get-tuple-element.10.routes, f32[1024,128]{1,0:T(8,128)S(1)} %bitcast.5, f32[64,128]{1,0:T(8,128)S(1)} %copy-done, f32[64,128]{1,0:T(8,128)S(1)} %collective-permute-done.other.refs_1_, f32[128,128]{1,0:T(8,128)S(1)} %collective-permute-done.1.refs_2_.refs_0_, ...), custom_call_target="tpu_custom_call" | custom-call | tf_op jit(solution)/shard_map/pallas_call | solution.py:264
  23.1 16.2 %all_to_all.10 = f32[16,80,128]{2,1,0:T(8,128)S(1)} all-to-all(f32[16,80,128]{2,1,0:T(8,128)S(1)} %bitcast.4), channel_id=1, replica_groups=mesh['prow'=16,'pcol'=8] {'prow'}, dimensions={0} | all-to-all | bytes 1310720 | tf_op jit(solution)/shard_map/all_to_all | solution.py:467
  39.3 6.6 %shard_map.41 = f32[1024,2048]{1,0:T(8,128)} custom-call(s32[1,128]{1,0:T(1,128)S(1)} %get-tuple-element.9.owned, f32[1280,128]{1,0:T(8,128)S(1)} %bitcast.3, f32[64,128]{1,0:T(8,128)S(1)} %copy-done, f32[64,128]{1,0:T(8,128)S(1)} %collective-permute-done.other.refs_1_, f32[128,128]{1,0:T(8,128)S(1)} %collective-permute-done.1.refs_2_.refs_0_, ...), custom_call_target="tpu_custom_call" | custom-call | tf_op jit(solution)/shard_map/pallas_call | solution.py:433
  (1 shorter events, 0.0 us)
Async XLA Ops:
  0.0 10.4 %copy-start = (f32[64,128]{1,0:T(8,128)S(1)}, f32[64,128]{1,0:T(8,128)}, u32[]{:S(2)}) copy-start(f32[64,128]{1,0:T(8,128)} %mine.3) | copy-start | bytes 98308
  0.0 17.0 %copy-start.1 = (s32[64]{0:T(128)S(1)}, s32[64]{0:T(128)}, u32[]{:S(2)}) copy-start(s32[64]{0:T(128)} %pivots.3) | copy-start | bytes 772
  0.0 3.3 %collective-permute-start = (f32[64,128]{1,0:T(8,128)}, f32[64,128]{1,0:T(8,128)S(1)}, u32[]{:S(2)}, u32[]{:S(2)}) collective-permute-start(f32[64,128]{1,0:T(8,128)} %mine.3), channel_id=1, source_target_pairs={{0,1},{1,0},{2,3},{3,2},{4,5},{5,4},{6,7},{7,6},{8,9},{9,8},{10,11... | collective-permute-start | bytes 98312 | tf_op jit(solution)/shard_map/ppermute | solution.py:460
  3.3 19.1 %all-to-all-start = ((f32[16,64,128]{2,1,0:T(8,128)}), f32[16,64,128]{2,1,0:T(8,128)S(1)}, u32[]{:S(2)}, u32[]{:S(2)}) async-start(f32[16,64,128]{2,1,0:T(8,128)} %shard_map.38), calls=%async_computation | async-start | bytes 1048576 | tf_op jit(solution)/shard_map/all_to_all | solution.py:463
  10.5 8.8 %collective-permute-start.3 = (f32[128,128]{1,0:T(8,128)S(1)}, f32[128,128]{1,0:T(8,128)S(1)}, u32[]{:S(2)}, u32[]{:S(2)}) collective-permute-start(f32[128,128]{1,0:T(8,128)S(1)} %shard_map.39), channel_id=1, source_target_pairs={{0,2},{1,3},{2,4},{3,5},{4,6},{5,7},{6,0},{7,1},{8,10},{9,11},{10,... | collective-permute-start | bytes 196616 | tf_op jit(solution)/shard_map/ppermute | solution.py:464
  12.4 7.0 %collective-permute-start.2 = (f32[128,128]{1,0:T(8,128)S(1)}, f32[128,128]{1,0:T(8,128)S(1)}, u32[]{:S(2)}, u32[]{:S(2)}) collective-permute-start(f32[128,128]{1,0:T(8,128)S(1)} %shard_map.39), channel_id=1, source_target_pairs={{0,4},{1,5},{2,6},{3,7},{4,0},{5,1},{6,2},{7,3},{8,12},{9,13},{10,... | collective-permute-start | bytes 196616 | tf_op jit(solution)/shard_map/ppermute | solution.py:464
  16.0 4.3 %collective-permute-start.1 = (f32[128,128]{1,0:T(8,128)S(1)}, f32[128,128]{1,0:T(8,128)S(1)}, u32[]{:S(2)}, u32[]{:S(2)}) collective-permute-start(f32[128,128]{1,0:T(8,128)S(1)} %shard_map.39), channel_id=1, source_target_pairs={{0,6},{1,7},{2,0},{3,1},{4,2},{5,3},{6,4},{7,5},{8,14},{9,15},{10,... | collective-permute-start | bytes 196616 | tf_op jit(solution)/shard_map/ppermute | solution.py:464

commit v7 on v6

--- a/solution.py
+++ b/solution.py
@@ -299,7 +299,7 @@
 ):
     pairs, refs = refs[:3], refs[3:]
     trailing, updated, block, kept, chosen, tops_here, multipliers, own, columns = refs[:9]
-    arrive, leave, sem, row_sem = refs[9:]
+    uppers, factors, arrive, leave, sem, row_sem = refs[9:]
     me = lax.axis_index("prow")
 
     def load(k):
@@ -375,24 +375,33 @@
     left = jnp.concatenate([inv_high, inv_mid, inv_low, inv_high, inv_mid, inv_high], axis=1)
 
     lax.fori_loop(0, n_away, fetched, 0)
-    for k, (start, width) in enumerate(CHUNKS):
+    for start, width in CHUNKS:
         cols = slice(start, start + width)
         pieces = range(start // LANES, (start + width) // LANES)
-        parts = [slice(p * LANES, (p + 1) * LANES) for p in pieces]
-        load(k).wait()
         tops = jnp.concatenate(
             [
-                jnp.where(chosen[...] > 0, kept[:, part], given[p * BACK : p * BACK + NB, :])
-                for p, part in zip(pieces, parts)
+                jnp.where(
+                    chosen[...] > 0,
+                    kept[:, p * LANES : (p + 1) * LANES],
+                    given[p * BACK : p * BACK + NB, :],
+                )
+                for p in pieces
             ],
             axis=1,
         )
         high, mid, low = thirds(tops)
         right = jnp.concatenate([high, high, high, mid, mid, low], axis=0)
         upper = jnp.dot(left, right, preferred_element_type=F32)
+        uppers[:, cols] = upper
         up_high, up_low = halves(upper)
-        factor = jnp.concatenate([up_high, up_high, up_low, up_low], axis=0)
-        product = jnp.dot(multipliers[...], factor, preferred_element_type=F32)
+        factors[:, cols] = jnp.concatenate([up_high, up_high, up_low, up_low], axis=0)
+
+    for k, (start, width) in enumerate(CHUNKS):
+        cols = slice(start, start + width)
+        pieces = range(start // LANES, (start + width) // LANES)
+        parts = [slice(p * LANES, (p + 1) * LANES) for p in pieces]
+        product = jnp.dot(multipliers[...], factors[:, cols], preferred_element_type=F32)
+        load(k).wait()
 
         def displace(i, carry):
             row, j = own[0, 1 + i] // NB, own[0, 1 + i] % NB
@@ -421,7 +430,7 @@
 
         @pl.when(me == 0)
         def _():
-            block[0:NB, cols] = upper
+            block[0:NB, cols] = uppers[:, cols]
 
         store(k).start()
     for k in range(len(CHUNKS)):
@@ -443,6 +452,8 @@
             pltpu.VMEM((rows, 4 * NB), BF16),
             pltpu.SMEM((1, OWN), jnp.int32),
             pltpu.VMEM((NB, NB, LANES), F32),
+            pltpu.VMEM((NB, cols), F32),
+            pltpu.VMEM((4 * NB, cols), BF16),
             pltpu.SemaphoreType.DMA((len(CHUNKS),)),
             pltpu.SemaphoreType.DMA((len(CHUNKS),)),
             pltpu.SemaphoreType.DMA,

time: 46.4 us -> 45.8 us (0.987)
  no operation moved by 1% of the time
where the time goes in v7:
time: 45.8 us; the launch traced here: 45.4 us
  blocking collectives  16.2 us (35%)
  starting transfers between devices  13.5 us (29%)
  Pallas kernels  12.4 us (27%)
  waiting for transfers between devices  3.23 us (7%)
    all_to_all x1, blocking collectives, body(): given = lax.all_to_all(back.reshape(N_PROW, BACK, LANES), 'prow', 0, 0)  16.2 us
    all_to_all x1, starting transfers between devices, body(): got = lax.all_to_all(sent, 'prow', 0, 0)  6.97 us
    ppermute x3, starting transfers between devices, body(): lax.ppermute(pair, 'pcol', ring(4 - turn))  6.58 us
    pallas_call x1, Pallas kernels, update(): pl.pallas_call(update_kernel, out_shape=jax.ShapeDtypeStruct((rows, cols)...  6.23 us
    pallas_call x1, Pallas kernels, pick(): pl.pallas_call(pick_kernel, out_shape=jax.ShapeDtypeStruct((N_PROW, NB, L...  3.37 us
    pallas_call x1, Pallas kernels, route(): pl.pallas_call(route_kernel, out_shape=(jax.ShapeDtypeStruct((1, ROUTES),...  2.16 us
    all_to_all x1, waiting for transfers between devices, body(): got = lax.all_to_all(sent, 'prow', 0, 0)  2.14 us
    ppermute x3, waiting for transfers between devices, body(): lax.ppermute(pair, 'pcol', ring(4 - turn))  1.08 us
  transfers between devices with their start and end apart: 5, of which 3 were waited for; matrix products, arithmetic and copies ran while one was open for 0% of the time, Pallas kernels for 12%

profile of v7, /device:TPU:0, one launch (start us, length us, event | category | flops | bytes accessed | tf_op | source)
XLA Modules:
  0.0 45.4 jit_solution(6718199394623743301)
XLA Ops:
  0.0 0.0 copy-start
  0.0 0.0 copy-start.1
  0.0 0.0 collective-permute-start
  0.0 3.4 %shard_map.38 = f32[16,64,128]{2,1,0:T(8,128)} custom-call(s32[64]{0:T(128)} %pivots.3, f32[1024,2048]{1,0:T(8,128)} %refs_3_.1), custom_call_target="tpu_custom_call" | custom-call | tf_op jit(solution)/shard_map/pallas_call | solution.py:116
  3.4 0.0 collective-permute-done.other.refs_1_
  3.4 7.0 %all-to-all-start = ((f32[16,64,128]{2,1,0:T(8,128)}), f32[16,64,128]{2,1,0:T(8,128)S(1)}, u32[]{:S(2)}, u32[]{:S(2)}) async-start(f32[16,64,128]{2,1,0:T(8,128)} %shard_map.38), calls=%async_computation | async-start | bytes 1048576 | tf_op jit(solution)/shard_map/all_to_all | solution.py:474
  10.4 0.0 copy-done
  10.4 2.0 %collective-permute-start.3 = (f32[128,128]{1,0:T(8,128)S(1)}, f32[128,128]{1,0:T(8,128)S(1)}, u32[]{:S(2)}, u32[]{:S(2)}) collective-permute-start(f32[128,128]{1,0:T(8,128)S(1)} %shard_map.39), channel_id=1, source_target_pairs={{0,2},{1,3},{2,4},{3,5},{4,6},{5,7},{6,0},{7,1},{8,10},{9,11},{10,... | collective-permute-start | bytes 196616 | tf_op jit(solution)/shard_map/ppermute | solution.py:475
  12.4 3.6 %collective-permute-start.2 = (f32[128,128]{1,0:T(8,128)S(1)}, f32[128,128]{1,0:T(8,128)S(1)}, u32[]{:S(2)}, u32[]{:S(2)}) collective-permute-start(f32[128,128]{1,0:T(8,128)S(1)} %shard_map.39), channel_id=1, source_target_pairs={{0,4},{1,5},{2,6},{3,7},{4,0},{5,1},{6,2},{7,3},{8,12},{9,13},{10,... | collective-permute-start | bytes 196616 | tf_op jit(solution)/shard_map/ppermute | solution.py:475
  16.0 1.0 %collective-permute-start.1 = (f32[128,128]{1,0:T(8,128)S(1)}, f32[128,128]{1,0:T(8,128)S(1)}, u32[]{:S(2)}, u32[]{:S(2)}) collective-permute-start(f32[128,128]{1,0:T(8,128)S(1)} %shard_map.39), channel_id=1, source_target_pairs={{0,6},{1,7},{2,0},{3,1},{4,2},{5,3},{6,4},{7,5},{8,14},{9,15},{10,... | collective-permute-start | bytes 196616 | tf_op jit(solution)/shard_map/ppermute | solution.py:475
  17.0 0.0 copy-done.1
  17.0 2.2 %shard_map.37 = (s32[1,192]{1,0:T(1,128)S(1)}, s32[1,128]{1,0:T(1,128)S(1)}) custom-call(s32[64]{0:T(128)S(1)} %copy-done.1), custom_call_target="tpu_custom_call" | custom-call | tf_op jit(solution)/shard_map/pallas_call | solution.py:186
  19.1 0.0 collective-permute-done.3.refs_4_.refs_2_
  19.2 0.3 collective-permute-done.2.refs_3_.refs_1_
  19.4 0.8 %collective-permute-done.1.refs_2_.refs_0_ = f32[128,128]{1,0:T(8,128)S(1)} collective-permute-done((f32[128,128]{1,0:T(8,128)S(1)}, f32[128,128]{1,0:T(8,128)S(1)}, u32[]{:S(2)}, u32[]{:S(2)}) %collective-permute-start.1) | collective-permute-done | bytes 65568 | tf_op jit(solution)/shard_map/ppermute | solution.py:475
  20.2 2.1 %all-to-all-done = f32[16,64,128]{2,1,0:T(8,128)S(1)} async-done(((f32[16,64,128]{2,1,0:T(8,128)}), f32[16,64,128]{2,1,0:T(8,128)S(1)}, u32[]{:S(2)}, u32[]{:S(2)}) %all-to-all-start) | async-done | bytes 524320 | tf_op jit(solution)/shard_map/all_to_all | solution.py:474
  22.4 0.7 %shard_map.40 = f32[1280,128]{1,0:T(8,128)S(1)} custom-call(s32[1,192]{1,0:T(1,128)S(1)} %get-tuple-element.10.routes, f32[1024,128]{1,0:T(8,128)S(1)} %bitcast.5, f32[64,128]{1,0:T(8,128)S(1)} %copy-done, f32[64,128]{1,0:T(8,128)S(1)} %collective-permute-done.other.refs_1_, f32[128,128]{1,0:T(8,128)S(1)} %collective-permute-done.1.refs_2_.refs_0_, ...), custom_call_target="tpu_custom_call" | custom-call | tf_op jit(solution)/shard_map/pallas_call | solution.py:264
  23.1 16.2 %all_to_all.10 = f32[16,80,128]{2,1,0:T(8,128)S(1)} all-to-all(f32[16,80,128]{2,1,0:T(8,128)S(1)} %bitcast.4), channel_id=1, replica_groups=mesh['prow'=16,'pcol'=8] {'prow'}, dimensions={0} | all-to-all | bytes 1310720 | tf_op jit(solution)/shard_map/all_to_all | solution.py:478
  39.2 6.2 %shard_map.41 = f32[1024,2048]{1,0:T(8,128)} custom-call(s32[1,128]{1,0:T(1,128)S(1)} %get-tuple-element.9.owned, f32[1280,128]{1,0:T(8,128)S(1)} %bitcast.3, f32[64,128]{1,0:T(8,128)S(1)} %copy-done, f32[64,128]{1,0:T(8,128)S(1)} %collective-permute-done.other.refs_1_, f32[128,128]{1,0:T(8,128)S(1)} %collective-permute-done.1.refs_2_.refs_0_, ...), custom_call_target="tpu_custom_call" | custom-call | tf_op jit(solution)/shard_map/pallas_call | solution.py:442
  (1 shorter events, 0.0 us)
Async XLA Ops:
  0.0 10.4 %copy-start = (f32[64,128]{1,0:T(8,128)S(1)}, f32[64,128]{1,0:T(8,128)}, u32[]{:S(2)}) copy-start(f32[64,128]{1,0:T(8,128)} %mine.3) | copy-start | bytes 98308
  0.0 17.0 %copy-start.1 = (s32[64]{0:T(128)S(1)}, s32[64]{0:T(128)}, u32[]{:S(2)}) copy-start(s32[64]{0:T(128)} %pivots.3) | copy-start | bytes 772
  0.0 3.4 %collective-permute-start = (f32[64,128]{1,0:T(8,128)}, f32[64,128]{1,0:T(8,128)S(1)}, u32[]{:S(2)}, u32[]{:S(2)}) collective-permute-start(f32[64,128]{1,0:T(8,128)} %mine.3), channel_id=1, source_target_pairs={{0,1},{1,0},{2,3},{3,2},{4,5},{5,4},{6,7},{7,6},{8,9},{9,8},{10,11... | collective-permute-start | bytes 98312 | tf_op jit(solution)/shard_map/ppermute | solution.py:471
  3.4 19.0 %all-to-all-start = ((f32[16,64,128]{2,1,0:T(8,128)}), f32[16,64,128]{2,1,0:T(8,128)S(1)}, u32[]{:S(2)}, u32[]{:S(2)}) async-start(f32[16,64,128]{2,1,0:T(8,128)} %shard_map.38), calls=%async_computation | async-start | bytes 1048576 | tf_op jit(solution)/shard_map/all_to_all | solution.py:474
  10.4 8.8 %collective-permute-start.3 = (f32[128,128]{1,0:T(8,128)S(1)}, f32[128,128]{1,0:T(8,128)S(1)}, u32[]{:S(2)}, u32[]{:S(2)}) collective-permute-start(f32[128,128]{1,0:T(8,128)S(1)} %shard_map.39), channel_id=1, source_target_pairs={{0,2},{1,3},{2,4},{3,5},{4,6},{5,7},{6,0},{7,1},{8,10},{9,11},{10,... | collective-permute-start | bytes 196616 | tf_op jit(solution)/shard_map/ppermute | solution.py:475
  12.4 7.0 %collective-permute-start.2 = (f32[128,128]{1,0:T(8,128)S(1)}, f32[128,128]{1,0:T(8,128)S(1)}, u32[]{:S(2)}, u32[]{:S(2)}) collective-permute-start(f32[128,128]{1,0:T(8,128)S(1)} %shard_map.39), channel_id=1, source_target_pairs={{0,4},{1,5},{2,6},{3,7},{4,0},{5,1},{6,2},{7,3},{8,12},{9,13},{10,... | collective-permute-start | bytes 196616 | tf_op jit(solution)/shard_map/ppermute | solution.py:475
  16.0 4.3 %collective-permute-start.1 = (f32[128,128]{1,0:T(8,128)S(1)}, f32[128,128]{1,0:T(8,128)S(1)}, u32[]{:S(2)}, u32[]{:S(2)}) collective-permute-start(f32[128,128]{1,0:T(8,128)S(1)} %shard_map.39), channel_id=1, source_target_pairs={{0,6},{1,7},{2,0},{3,1},{4,2},{5,3},{6,4},{7,5},{8,14},{9,15},{10,... | collective-permute-start | bytes 196616 | tf_op jit(solution)/shard_map/ppermute | solution.py:475

commit v8 on v7

--- a/solution.py
+++ b/solution.py
@@ -313,7 +313,6 @@
     copy = pltpu.make_async_copy(owned, own, sem)
     copy.start()
     load(0).start()
-    load(1).start()
 
     copy.wait()
     n_own = own[0, 0]
@@ -342,7 +341,7 @@
 
     chosen[...] = jnp.zeros_like(chosen)
     lax.fori_loop(0, n_away, fetch, 0)
-    for k in range(2, len(CHUNKS)):
+    for k in range(1, len(CHUNKS)):
         load(k).start()
 
     c = lax.axis_index("pcol")

time: 45.8 us -> 46.1 us (level)
  no operation moved by 1% of the time
where the time goes in v8:
time: 46.1 us; the launch traced here: 45.7 us
  blocking collectives  16.2 us (35%)
  starting transfers between devices  13.8 us (30%)
  Pallas kernels  12.4 us (27%)
  waiting for transfers between devices  3.23 us (7%)
    all_to_all x1, blocking collectives, body(): given = lax.all_to_all(back.reshape(N_PROW, BACK, LANES), 'prow', 0, 0)  16.2 us
    all_to_all x1, starting transfers between devices, body(): got = lax.all_to_all(sent, 'prow', 0, 0)  7.22 us
    ppermute x3, starting transfers between devices, body(): lax.ppermute(pair, 'pcol', ring(4 - turn))  6.58 us
    pallas_call x1, Pallas kernels, update(): pl.pallas_call(update_kernel, out_shape=jax.ShapeDtypeStruct((rows, cols)...  6.23 us
    pallas_call x1, Pallas kernels, pick(): pl.pallas_call(pick_kernel, out_shape=jax.ShapeDtypeStruct((N_PROW, NB, L...  3.37 us
    pallas_call x1, Pallas kernels, route(): pl.pallas_call(route_kernel, out_shape=(jax.ShapeDtypeStruct((1, ROUTES),...  2.16 us
    all_to_all x1, waiting for transfers between devices, body(): got = lax.all_to_all(sent, 'prow', 0, 0)  2.14 us
    ppermute x3, waiting for transfers between devices, body(): lax.ppermute(pair, 'pcol', ring(4 - turn))  1.08 us
  transfers between devices with their start and end apart: 5, of which 3 were waited for; matrix products, arithmetic and copies ran while one was open for 0% of the time, Pallas kernels for 12%

profile of v8, /device:TPU:0, one launch (start us, length us, event | category | flops | bytes accessed | tf_op | source)
XLA Modules:
  0.0 45.7 jit_solution(5684697978803534325)
XLA Ops:
  0.0 0.0 copy-start
  0.0 0.0 copy-start.1
  0.0 0.0 collective-permute-start
  0.0 3.4 %shard_map.38 = f32[16,64,128]{2,1,0:T(8,128)} custom-call(s32[64]{0:T(128)} %pivots.3, f32[1024,2048]{1,0:T(8,128)} %refs_3_.1), custom_call_target="tpu_custom_call" | custom-call | tf_op jit(solution)/shard_map/pallas_call | solution.py:116
  3.4 0.0 collective-permute-done.other.refs_1_
  3.4 7.2 %all-to-all-start = ((f32[16,64,128]{2,1,0:T(8,128)}), f32[16,64,128]{2,1,0:T(8,128)S(1)}, u32[]{:S(2)}, u32[]{:S(2)}) async-start(f32[16,64,128]{2,1,0:T(8,128)} %shard_map.38), calls=%async_computation | async-start | bytes 1048576 | tf_op jit(solution)/shard_map/all_to_all | solution.py:473
  10.6 0.0 copy-done
  10.6 2.0 %collective-permute-start.3 = (f32[128,128]{1,0:T(8,128)S(1)}, f32[128,128]{1,0:T(8,128)S(1)}, u32[]{:S(2)}, u32[]{:S(2)}) collective-permute-start(f32[128,128]{1,0:T(8,128)S(1)} %shard_map.39), channel_id=1, source_target_pairs={{0,2},{1,3},{2,4},{3,5},{4,6},{5,7},{6,0},{7,1},{8,10},{9,11},{10,... | collective-permute-start | bytes 196616 | tf_op jit(solution)/shard_map/ppermute | solution.py:474
  12.6 3.6 %collective-permute-start.2 = (f32[128,128]{1,0:T(8,128)S(1)}, f32[128,128]{1,0:T(8,128)S(1)}, u32[]{:S(2)}, u32[]{:S(2)}) collective-permute-start(f32[128,128]{1,0:T(8,128)S(1)} %shard_map.39), channel_id=1, source_target_pairs={{0,4},{1,5},{2,6},{3,7},{4,0},{5,1},{6,2},{7,3},{8,12},{9,13},{10,... | collective-permute-start | bytes 196616 | tf_op jit(solution)/shard_map/ppermute | solution.py:474
  16.2 1.0 %collective-permute-start.1 = (f32[128,128]{1,0:T(8,128)S(1)}, f32[128,128]{1,0:T(8,128)S(1)}, u32[]{:S(2)}, u32[]{:S(2)}) collective-permute-start(f32[128,128]{1,0:T(8,128)S(1)} %shard_map.39), channel_id=1, source_target_pairs={{0,6},{1,7},{2,0},{3,1},{4,2},{5,3},{6,4},{7,5},{8,14},{9,15},{10,... | collective-permute-start | bytes 196616 | tf_op jit(solution)/shard_map/ppermute | solution.py:474
  17.2 0.0 copy-done.1
  17.2 2.2 %shard_map.37 = (s32[1,192]{1,0:T(1,128)S(1)}, s32[1,128]{1,0:T(1,128)S(1)}) custom-call(s32[64]{0:T(128)S(1)} %copy-done.1), custom_call_target="tpu_custom_call" | custom-call | tf_op jit(solution)/shard_map/pallas_call | solution.py:186
  19.4 0.0 collective-permute-done.3.refs_4_.refs_2_
  19.4 0.3 collective-permute-done.2.refs_3_.refs_1_
  19.7 0.8 %collective-permute-done.1.refs_2_.refs_0_ = f32[128,128]{1,0:T(8,128)S(1)} collective-permute-done((f32[128,128]{1,0:T(8,128)S(1)}, f32[128,128]{1,0:T(8,128)S(1)}, u32[]{:S(2)}, u32[]{:S(2)}) %collective-permute-start.1) | collective-permute-done | bytes 65568 | tf_op jit(solution)/shard_map/ppermute | solution.py:474
  20.5 2.1 %all-to-all-done = f32[16,64,128]{2,1,0:T(8,128)S(1)} async-done(((f32[16,64,128]{2,1,0:T(8,128)}), f32[16,64,128]{2,1,0:T(8,128)S(1)}, u32[]{:S(2)}, u32[]{:S(2)}) %all-to-all-start) | async-done | bytes 524320 | tf_op jit(solution)/shard_map/all_to_all | solution.py:473
  22.6 0.7 %shard_map.40 = f32[1280,128]{1,0:T(8,128)S(1)} custom-call(s32[1,192]{1,0:T(1,128)S(1)} %get-tuple-element.10.routes, f32[1024,128]{1,0:T(8,128)S(1)} %bitcast.5, f32[64,128]{1,0:T(8,128)S(1)} %copy-done, f32[64,128]{1,0:T(8,128)S(1)} %collective-permute-done.other.refs_1_, f32[128,128]{1,0:T(8,128)S(1)} %collective-permute-done.1.refs_2_.refs_0_, ...), custom_call_target="tpu_custom_call" | custom-call | tf_op jit(solution)/shard_map/pallas_call | solution.py:264
  23.3 16.2 %all_to_all.10 = f32[16,80,128]{2,1,0:T(8,128)S(1)} all-to-all(f32[16,80,128]{2,1,0:T(8,128)S(1)} %bitcast.4), channel_id=1, replica_groups=mesh['prow'=16,'pcol'=8] {'prow'}, dimensions={0} | all-to-all | bytes 1310720 | tf_op jit(solution)/shard_map/all_to_all | solution.py:477
  39.5 6.2 %shard_map.41 = f32[1024,2048]{1,0:T(8,128)} custom-call(s32[1,128]{1,0:T(1,128)S(1)} %get-tuple-element.9.owned, f32[1280,128]{1,0:T(8,128)S(1)} %bitcast.3, f32[64,128]{1,0:T(8,128)S(1)} %copy-done, f32[64,128]{1,0:T(8,128)S(1)} %collective-permute-done.other.refs_1_, f32[128,128]{1,0:T(8,128)S(1)} %collective-permute-done.1.refs_2_.refs_0_, ...), custom_call_target="tpu_custom_call" | custom-call | tf_op jit(solution)/shard_map/pallas_call | solution.py:441
  (1 shorter events, 0.0 us)
Async XLA Ops:
  0.0 10.6 %copy-start = (f32[64,128]{1,0:T(8,128)S(1)}, f32[64,128]{1,0:T(8,128)}, u32[]{:S(2)}) copy-start(f32[64,128]{1,0:T(8,128)} %mine.3) | copy-start | bytes 98308
  0.0 17.2 %copy-start.1 = (s32[64]{0:T(128)S(1)}, s32[64]{0:T(128)}, u32[]{:S(2)}) copy-start(s32[64]{0:T(128)} %pivots.3) | copy-start | bytes 772
  0.0 3.4 %collective-permute-start = (f32[64,128]{1,0:T(8,128)}, f32[64,128]{1,0:T(8,128)S(1)}, u32[]{:S(2)}, u32[]{:S(2)}) collective-permute-start(f32[64,128]{1,0:T(8,128)} %mine.3), channel_id=1, source_target_pairs={{0,1},{1,0},{2,3},{3,2},{4,5},{5,4},{6,7},{7,6},{8,9},{9,8},{10,11... | collective-permute-start | bytes 98312 | tf_op jit(solution)/shard_map/ppermute | solution.py:470
  3.4 19.2 %all-to-all-start = ((f32[16,64,128]{2,1,0:T(8,128)}), f32[16,64,128]{2,1,0:T(8,128)S(1)}, u32[]{:S(2)}, u32[]{:S(2)}) async-start(f32[16,64,128]{2,1,0:T(8,128)} %shard_map.38), calls=%async_computation | async-start | bytes 1048576 | tf_op jit(solution)/shard_map/all_to_all | solution.py:473
  10.6 8.8 %collective-permute-start.3 = (f32[128,128]{1,0:T(8,128)S(1)}, f32[128,128]{1,0:T(8,128)S(1)}, u32[]{:S(2)}, u32[]{:S(2)}) collective-permute-start(f32[128,128]{1,0:T(8,128)S(1)} %shard_map.39), channel_id=1, source_target_pairs={{0,2},{1,3},{2,4},{3,5},{4,6},{5,7},{6,0},{7,1},{8,10},{9,11},{10,... | collective-permute-start | bytes 196616 | tf_op jit(solution)/shard_map/ppermute | solution.py:474
  12.6 7.0 %collective-permute-start.2 = (f32[128,128]{1,0:T(8,128)S(1)}, f32[128,128]{1,0:T(8,128)S(1)}, u32[]{:S(2)}, u32[]{:S(2)}) collective-permute-start(f32[128,128]{1,0:T(8,128)S(1)} %shard_map.39), channel_id=1, source_target_pairs={{0,4},{1,5},{2,6},{3,7},{4,0},{5,1},{6,2},{7,3},{8,12},{9,13},{10,... | collective-permute-start | bytes 196616 | tf_op jit(solution)/shard_map/ppermute | solution.py:474
  16.2 4.3 %collective-permute-start.1 = (f32[128,128]{1,0:T(8,128)S(1)}, f32[128,128]{1,0:T(8,128)S(1)}, u32[]{:S(2)}, u32[]{:S(2)}) collective-permute-start(f32[128,128]{1,0:T(8,128)S(1)} %shard_map.39), channel_id=1, source_target_pairs={{0,6},{1,7},{2,0},{3,1},{4,2},{5,3},{6,4},{7,5},{8,14},{9,15},{10,... | collective-permute-start | bytes 196616 | tf_op jit(solution)/shard_map/ppermute | solution.py:474
